TPU v7x, 128 devices: a whole 4x4x4 slice. The times are simulated.
128 devices in a mesh: dp: 8 (over x, core), tensor: 16 (over y, z).
Axes of the slice: x: 4, y: 4, z: 4, core: 2. Of those that a mesh axis runs over, the one named last changes fastest.
Arguments:
- text_hidden: bfloat16 [2048, 8192], P('dp', 'tensor'), may hold values from -6 to 6
- norm_gain: bfloat16 [8192], P('tensor'), may hold values from 0.5 to 1.5
- gate_alpha: float32 [8192], P('tensor'), may hold values from 0.3 to 1.5
- latents: bfloat16 [8, 64, 8192], P('dp', None, 'tensor'), may hold values from -6 to 6
- query_weight: bfloat16 [8192, 4096], P(None, 'tensor'), may hold values from -0.0625 to 0.0625
- key_weight: bfloat16 [8192, 4096], P(None, 'tensor'), may hold values from -0.0625 to 0.0625
- value_weight: bfloat16 [8192, 4096], P(None, 'tensor'), may hold values from -0.0625 to 0.0625
- out_weight: bfloat16 [4096, 8192], P('tensor'), may hold values from -0.375 to 0.375
- citations: int32 [16, 4], P('dp'), may hold values from 0 to 7, all different within a row
- image_slot: int32 [8], replicated, may hold values from 0 to 7, each once
- out_grad: bfloat16 [2048, 8192], P('dp', 'tensor'), may hold values from -6 to 6
Outputs:
- layer_out: bfloat16 [2048, 8192], P('dp', 'tensor')
- text_grad: bfloat16 [2048, 8192], P('dp', 'tensor')
- query_weight_grad: bfloat16 [8192, 4096], P('dp', 'tensor')
- key_weight_grad: bfloat16 [8192, 4096], P('dp', 'tensor')
- value_weight_grad: bfloat16 [8192, 4096], P('dp', 'tensor')
- out_weight_grad: bfloat16 [4096, 8192], P('tensor', 'dp')
- gain_grad: float32 [8192], P('tensor')
- gate_grad: float32 [8192], P('tensor')
Inputs may be any that keep to these rules, and one draw needn't show every extreme that they name: `citations`: each row lists 4 different image ids; every image id is cited by some span. `image_slot`: a permutation; image id i is held in slot image_slot[i] of latents.
All inputs are finite; a program needn't handle non-finite values.
Results may differ from a plain program's by a relative error of at most 0.02.
Values may be sent and summed in bfloat16 or wider, within the bound.
No kernel may reach another device: no remote copies, remote signals or barrier semaphores. Data moves between devices by JAX's collectives and lax.ppermute only.
A program may use at most 128 MiB of HBM per device.

v0:
```python
import functools

import jax
import jax.numpy as jnp
from jax import lax
from jax.experimental import pallas as pl
from jax.experimental.pallas import tpu as pltpu
from jax.sharding import PartitionSpec as P

D = 8192
HEAD_DIM = 128
SIDE = 4
CORES = 2
LAT = 64
ROWS = 256
WIDTH = 512
COLS = 256
EXTRA = 16
EPSILON = 1e-05
SCALE = HEAD_DIM ** (-0.5)

BF = jnp.bfloat16
F32 = jnp.float32


def dot(left, right, over):
    return lax.dot_general(left, right, ((over[:1], over[1:]), ((), ())), preferred_element_type=F32)


def send_z(value, by):
    pairs = [(t, t // SIDE * SIDE + (t + by) % SIDE) for t in range(SIDE * SIDE)]
    return lax.ppermute(value, "tensor", pairs)


def send_y(value, by):
    pairs = [(t, (t + by * SIDE) % (SIDE * SIDE)) for t in range(SIDE * SIDE)]
    return lax.ppermute(value, "tensor", pairs)


def send_x(value, by):
    count = SIDE * CORES
    return lax.ppermute(value, "dp", [(i, (i + by * CORES) % count) for i in range(count)])


def send_core(value):
    return lax.ppermute(value, "dp", [(i, i ^ 1) for i in range(SIDE * CORES)])


def send_latents_home(value):
    moves = []
    for i in range(8):
        for t in range(16):
            moves.append((i * 16 + t, (t // 2) * 16 + i * 2 + t % 2))
    return lax.ppermute(value, ("dp", "tensor"), moves)


def hold(*values):
    return lax.optimization_barrier(values)


def gather_direct(value, send):
    above, below, across = send(value, -1), send(value, 1), send(value, 2)
    return [value, above, across, below]


def add(*terms):
    total = terms[0].astype(F32)
    for term in terms[1:]:
        total = total + term.astype(F32)
    return total


def feature_block(pos, ky, kz):
    return lax.rem(pos[2] + ky, SIDE) * SIDE + lax.rem(pos[3] + kz, SIDE)


def call(body, pos, grid, ins, outs, scratch, flops, moved):
    arrays, in_specs = zip(*ins)
    shapes, out_specs = zip(*outs)
    return pl.pallas_call(
        body,
        grid_spec=pltpu.PrefetchScalarGridSpec(
            num_scalar_prefetch=1,
            grid=grid,
            in_specs=list(in_specs),
            out_specs=list(out_specs),
            scratch_shapes=scratch,
        ),
        out_shape=list(shapes),
        compiler_params=pltpu.CompilerParams(
            dimension_semantics=("arbitrary",) * len(grid), vmem_limit_bytes=40 * 2**20
        ),
        cost_estimate=pl.CostEstimate(flops=flops, bytes_accessed=moved, transcendentals=0),
    )(pos, *arrays)


def whole(array):
    zeros = (0,) * array.ndim
    return array, pl.BlockSpec(array.shape, lambda *_: zeros)


def whole_out(shape, dtype):
    zeros = (0,) * len(shape)
    return jax.ShapeDtypeStruct(shape, dtype), pl.BlockSpec(shape, lambda *_: zeros)


def query_body(count, first, last, pos, *refs):
    pieces, gains, weights = refs[:count], refs[count : 2 * count], refs[2 * count : 3 * count]
    rest = refs[3 * count :]
    if not first:
        total_in, squares_in, *rest = rest
    out_a, out_b, total, squares = rest
    step = pl.program_id(0)

    @pl.when(step == 0)
    def _():
        if first:
            total[...] = jnp.zeros_like(total)
            squares[...] = jnp.zeros_like(squares)
        else:
            total[...] = total_in[...]
            squares[...] = squares_in[...]

    for piece, gain, weight in zip(pieces, gains, weights):
        text = piece[0].astype(F32)
        square = text * text
        squares[...] += (square[:, :128] + square[:, 128:256]) + (
            square[:, 256:384] + square[:, 384:]
        )
        scaled = (text * gain[0][:1].astype(F32)).astype(BF)
        total[...] += dot(scaled, weight[...], (1, 0))

    @pl.when(step == pl.num_programs(0) - 1)
    def _():
        if last:
            mean = jnp.sum(squares[...], axis=1, keepdims=True) / D
            inverse = lax.rsqrt(mean + EPSILON)
            out_a[...] = (total[...] * inverse).astype(BF)
            out_b[...] = jnp.broadcast_to(inverse, out_b.shape)
        else:
            out_a[...] = total[...]
            out_b[...] = squares[...]


def query_part(pos, arrays, places, small, weight, carry, last):
    steps = arrays[0].shape[0]
    ins = [(a, pl.BlockSpec((1, ROWS, WIDTH), lambda i, pos: (i, 0, 0))) for a in arrays]
    for ky, kz in places:
        at = ky * SIDE + kz
        ins.append((small, pl.BlockSpec((1, EXTRA, WIDTH), lambda i, pos, at=at: (at + i, 4, 0))))
    for ky, kz in places:
        index = lambda i, pos, ky=ky, kz=kz: (feature_block(pos, ky, kz + i), 0)
        ins.append((weight, pl.BlockSpec((WIDTH, COLS), index)))
    ins += [whole(value) for value in carry]
    outs = [
        whole_out((ROWS, COLS), BF if last else F32),
        whole_out((ROWS, 128), F32),
    ]
    scratch = [pltpu.VMEM((ROWS, COLS), F32), pltpu.VMEM((ROWS, 128), F32)]
    body = functools.partial(query_body, len(arrays), not carry, last)
    work = steps * len(arrays)
    return call(body, pos, (steps,), ins, outs, scratch, work * 2 * ROWS * WIDTH * COLS, work * 2**19)


def grad_body(count, first, last, pos, *refs):
    pieces, weights, rest = refs[:count], refs[count : 2 * count], refs[2 * count :]
    if not first:
        total_in, *rest = rest
    out, total = rest
    step = pl.program_id(0)

    @pl.when(step == 0)
    def _():
        total[...] = jnp.zeros_like(total) if first else total_in[...]

    for piece, weight in zip(pieces, weights):
        total[...] += dot(piece[0], weight[...], (1, 1))

    @pl.when(step == pl.num_programs(0) - 1)
    def _():
        out[...] = total[...].astype(out.dtype)


def grad_part(pos, arrays, places, weight, carry, last):
    steps = arrays[0].shape[0]
    ins = [(a, pl.BlockSpec((1, ROWS, WIDTH), lambda i, pos: (i, 0, 0))) for a in arrays]
    for kz, ky in places:
        index = lambda i, pos, ky=ky, kz=kz: (0, feature_block(pos, ky + i, kz))
        ins.append((weight, pl.BlockSpec((COLS, WIDTH), index)))
    ins += [whole(value) for value in carry]
    outs = [whole_out((ROWS, COLS), BF if last else F32)]
    body = functools.partial(grad_body, len(arrays), not carry, last)
    work = steps * len(arrays)
    scratch = [pltpu.VMEM((ROWS, COLS), F32)]
    return call(body, pos, (steps,), ins, outs, scratch, work * 2 * ROWS * WIDTH * COLS, work * 2**19)


def pair_body(pos, small, *refs):
    keys, values, out, total = refs[:SIDE], refs[SIDE : 2 * SIDE], refs[-2], refs[-1]
    step = pl.program_id(0)

    @pl.when(step == 0)
    def _():
        total[...] = jnp.zeros_like(total)

    for kz in range(SIDE):
        latents = small[kz, :LAT]
        total[:, :COLS] += dot(latents, keys[kz][...], (1, 0))
        total[:, COLS:] += dot(latents, values[kz][...], (1, 0))

    @pl.when(step == SIDE - 1)
    def _():
        out[...] = total[...].astype(BF)


def own_pair(pos, small, key_weight, value_weight):
    rows = small.shape[1]
    ins = [(small, pl.BlockSpec((SIDE, rows, WIDTH), lambda i, pos: (i, 0, 0)))]
    for weight in (key_weight, value_weight):
        for kz in range(SIDE):
            index = lambda i, pos, kz=kz: (feature_block(pos, i, kz), 0)
            ins.append((weight, pl.BlockSpec((WIDTH, COLS), index)))
    outs = [whole_out((LAT, 2 * COLS), BF)]
    scratch = [pltpu.VMEM((LAT, 2 * COLS), F32)]
    return call(pair_body, pos, (SIDE,), ins, outs, scratch, 2 * LAT * D * 512, 10 * 2**20)[0]


def attention_body(slots, queries, grads, pair, attended, query_grad, kept, given, row_dot, part):
    part[...] = jnp.zeros_like(part)
    span = ROWS // 2
    ones = jnp.ones((8, COLS), F32)
    for c in range(2):
        rows = slice(c * span, (c + 1) * span)
        places = [slots[c * 4 + j] for j in range(4)]
        blocks = [pair[at] for at in places]
        product, key_grads, value_grads = [], [], []
        for h in range(2):
            cols = slice(h * HEAD_DIM, (h + 1) * HEAD_DIM)
            value_cols = slice(COLS + h * HEAD_DIM, COLS + (h + 1) * HEAD_DIM)
            keys = jnp.concatenate([block[:, cols] for block in blocks], 0)
            values = jnp.concatenate([block[:, value_cols] for block in blocks], 0)
            query, grad = queries[rows, cols], grads[rows, cols]
            scores = dot(query, keys, (1, 1)) * SCALE
            scores = jnp.exp(scores - jnp.max(scores, axis=1, keepdims=True))
            probs = scores / jnp.sum(scores, axis=1, keepdims=True)
            probs_low = probs.astype(BF)
            attended[rows, cols] = dot(probs_low, values, (1, 0)).astype(BF)
            probs_grad = dot(grad, values, (1, 1))
            inner = jnp.sum(probs * probs_grad, axis=1, keepdims=True)
            score_low = (probs * (probs_grad - inner) * SCALE).astype(BF)
            out = dot(score_low, keys, (1, 0)).astype(BF)
            query_grad[rows, cols] = out
            product.append(out.astype(F32) * query.astype(F32))
            key_grads.append(dot(score_low, query, (0, 0)))
            value_grads.append(dot(probs_low, grad, (0, 0)))
        pair_grad = jnp.concatenate(key_grads + value_grads, 1)
        for j in range(4):
            part[places[j]] += pair_grad[j * LAT : (j + 1) * LAT]
        line = lax.dot_general(
            ones,
            jnp.concatenate(product, 1),
            (((1,), (1,)), ((), ())),
            precision=lax.Precision.HIGHEST,
            preferred_element_type=F32,
        )
        row_dot[:, rows] = jnp.concatenate([line, line], 0).astype(BF)
    row_dot[:, ROWS:] = jnp.zeros((EXTRA, WIDTH - ROWS), BF)
    for kx in range(SIDE):
        kept[kx] = part[kx * CORES].astype(BF)
        given[kx] = part[kx * CORES + 1].astype(BF)


def attention(slots, queries, grads, pair):
    ins = [whole(queries), whole(grads), whole(pair)]
    outs = [
        whole_out((ROWS, COLS), BF),
        whole_out((ROWS, COLS), BF),
        whole_out((SIDE, LAT, 2 * COLS), BF),
        whole_out((SIDE, LAT, 2 * COLS), BF),
        whole_out((EXTRA, WIDTH), BF),
    ]
    scratch = [pltpu.VMEM((SIDE * CORES, LAT, 2 * COLS), F32)]
    return call(attention_body, slots, (1,), ins, outs, scratch, 4 * 10 * 2**23, 3 * 2**20)


def parts_body(count, over, pos, left, *refs):
    weights, rest = refs[:count], refs[count:]
    tail = None
    if len(rest) > count:
        tail, *rest = rest
    for weight, out in zip(weights, rest):
        out[0, :ROWS] = dot(left[...], weight[...], over).astype(BF)
        if tail is not None:
            out[0, ROWS:] = tail[...]


def branch_parts(pos, left, weight, steps, places):
    ins = [whole(left)]
    outs = []
    for ky, kz in places:
        index = lambda i, pos, ky=ky, kz=kz: (0, feature_block(pos, ky, kz + i))
        ins.append((weight, pl.BlockSpec((COLS, WIDTH), index)))
        shape = jax.ShapeDtypeStruct((steps, ROWS, WIDTH), BF)
        outs.append((shape, pl.BlockSpec((1, ROWS, WIDTH), lambda i, pos: (i, 0, 0))))
    body = functools.partial(parts_body, len(places), (1, 0))
    work = steps * len(places)
    return call(body, pos, (steps,), ins, outs, [], work * 2 * ROWS * WIDTH * COLS, work * 2**19)


def normed_parts(pos, left, tail, weight, steps, places):
    ins = [whole(left)]
    outs = []
    for kz, ky in places:
        index = lambda i, pos, ky=ky, kz=kz: (feature_block(pos, ky + i, kz), 0)
        ins.append((weight, pl.BlockSpec((WIDTH, COLS), index)))
        shape = jax.ShapeDtypeStruct((steps, ROWS + EXTRA, WIDTH), BF)
        outs.append((shape, pl.BlockSpec((1, ROWS + EXTRA, WIDTH), lambda i, pos: (i, 0, 0))))
    ins.append(whole(tail))
    body = functools.partial(parts_body, len(places), (1, 1))
    work = steps * len(places)
    return call(body, pos, (steps,), ins, outs, [], work * 2 * ROWS * WIDTH * COLS, work * 2**19)


def target_piece(pos, g, other):
    core = 1 - pos[1] if other else pos[1]
    ky = lax.rem(pos[0] + g // 2 + SIDE - pos[2], SIDE)
    kz = lax.rem(core * 2 + g % 2 + SIDE - pos[3], SIDE)
    return ky, kz


def out_weight_body(pos, attended, piece, out):
    out[0] = dot(attended[...], piece[0], (0, 0)).astype(BF)


def out_weight_terms(pos, attended, grads, other):
    def index(g, pos):
        ky, kz = target_piece(pos, g, other)
        return kz * SIDE + ky, 0, 0

    ins = [whole(attended), (grads, pl.BlockSpec((1, ROWS, WIDTH), index))]
    shape = jax.ShapeDtypeStruct((SIDE, COLS, 2 * WIDTH), BF)
    outs = [(shape, pl.BlockSpec((1, COLS, WIDTH), lambda g, pos: (g // 2, 0, g % 2)))]
    return call(out_weight_body, pos, (8,), ins, outs, [], 8 * 2**26, 8 * 2**19)[0]


def query_weight_body(pos, query_grad, inverse, gain, piece, out):
    scale = jnp.concatenate([inverse[...]] * 4, 1)
    normed = (piece[0].astype(F32) * scale * gain[0][:1].astype(F32)).astype(BF)
    out[0] = dot(normed, query_grad[...], (0, 0)).astype(BF)


def query_weight_terms(pos, query_grad, inverse, small, text, other):
    def place(g, pos):
        ky, kz = target_piece(pos, g, other)
        return ky * SIDE + kz

    ins = [
        whole(query_grad),
        whole(inverse),
        (small, pl.BlockSpec((1, EXTRA, WIDTH), lambda g, pos: (place(g, pos), 4, 0))),
        (text, pl.BlockSpec((1, ROWS, WIDTH), lambda g, pos: (place(g, pos), 0, 0))),
    ]
    shape = jax.ShapeDtypeStruct((SIDE, 2 * WIDTH, COLS), BF)
    outs = [(shape, pl.BlockSpec((1, WIDTH, COLS), lambda g, pos: (g // 2, g % 2, 0)))]
    return call(query_weight_body, pos, (8,), ins, outs, [], 8 * 2**26, 8 * 2**19)[0]


def latent_body(pos, latents, near, far, key_out, value_out):
    for half in range(2):
        left, right = [], []
        for kx in range(SIDE):
            for other in range(2):
                x = lax.rem(pos[0] + kx, SIDE)
                core = 1 - pos[1] if other else pos[1]
                source = (x * CORES + core) * 2 + half
                ky = lax.rem(source // SIDE + SIDE - pos[2], SIDE)
                kz = lax.rem(lax.rem(source, SIDE) + SIDE - pos[3], SIDE)
                left.append(latents[kz * SIDE + ky])
                right.append((far if other else near)[kx])
        total = dot(jnp.concatenate(left, 0), jnp.concatenate(right, 0), (0, 0)).astype(BF)
        rows = slice(half * WIDTH, (half + 1) * WIDTH)
        key_out[rows] = total[:, :COLS]
        value_out[rows] = total[:, COLS:]


def latent_terms(pos, latents, near, far):
    ins = [
        (latents, pl.BlockSpec((16, LAT, WIDTH), lambda i, pos: (0, ROWS // LAT, 0))),
        whole(near),
        whole(far),
    ]
    outs = [whole_out((2 * WIDTH, COLS), BF), whole_out((2 * WIDTH, COLS), BF)]
    return call(latent_body, pos, (1,), ins, outs, [], 2**30, 3 * 2**20)


def shards(
    text_hidden,
    norm_gain,
    gate_alpha,
    latents,
    query_weight,
    key_weight,
    value_weight,
    out_weight,
    citations,
    image_slot,
    out_grad,
):
    place, lane = lax.axis_index("dp"), lax.axis_index("tensor")
    x, core = place // CORES, place % CORES
    y, z = lane // SIDE, lane % SIDE
    pos = jnp.stack([x, core, y, z]).astype(jnp.int32)
    own_latents = latents.reshape(LAT, WIDTH)

    tanh_gate = jnp.tanh(gate_alpha)
    upstream = out_grad.astype(F32)
    own_branch_grad = (upstream * tanh_gate).astype(BF)
    cited = jnp.take(image_slot, citations, axis=0).reshape(-1)
    slots = (cited // CORES + SIDE - x) % SIDE * CORES + (cited + core) % CORES
    slots = slots.astype(jnp.int32)

    slice_latents = send_latents_home(own_latents)
    gain_rows = jnp.broadcast_to(norm_gain[None, :], (EXTRA, WIDTH))
    small = jnp.stack(gather_direct(jnp.concatenate([own_latents, gain_rows], 0), send_z))
    text = jnp.stack(gather_direct(text_hidden, send_z))
    grads = jnp.stack(gather_direct(jnp.concatenate([own_branch_grad, slice_latents], 0), send_y))
    small, text, grads = hold(small, text, grads)

    grads_above, grads_below = send_z(grads, -1), send_z(grads, 1)
    small = jnp.concatenate(gather_direct(small, send_y), 0)
    text_above, text_below = send_y(text, -1), send_y(text, 1)

    total = query_part(pos, [text], [(0, 0)], small, query_weight, (), False)
    grad_total = grad_part(pos, [grads], [(0, 0)], out_weight, (), False)
    pair = own_pair(pos, small, key_weight, value_weight)
    pair = jnp.stack([pair, send_core(pair)])

    grads_above, grads_below, text_above, text_below, pair, total, grad_total = hold(
        grads_above, grads_below, text_above, text_below, pair, total, grad_total
    )
    grads_low, grads_high = send_z(grads_below[:2], 1), send_z(grads_above[2:], -1)
    text_low, text_high = send_y(text_below[:2], 1), send_y(text_above[2:], -1)
    pair = jnp.concatenate(gather_direct(pair, send_x), 0)
    total = query_part(
        pos, [text_above, text_below], [(1, 0), (3, 0)], small, query_weight, total, False
    )
    grad_total = grad_part(
        pos, [grads_above, grads_below], [(1, 0), (3, 0)], out_weight, grad_total, False
    )
    queries, inverse = query_part(
        pos, [text_low, text_high], [(2, 0), (2, 2)], small, query_weight, total, True
    )
    attended_grad = grad_part(
        pos, [grads_low, grads_high], [(2, 0), (2, 2)], out_weight, grad_total, True
    )[0]
    all_text = jnp.concatenate([text, text_above, text_low, text_high, text_below], 0)
    all_grads = jnp.concatenate([grads, grads_above, grads_low, grads_high, grads_below], 0)

    attended, query_grad, pair_kept, pair_given, row_dot = attention(
        slots, queries, attended_grad, pair
    )

    branch_low, branch_high = branch_parts(pos, attended, out_weight, 2, [(2, 0), (2, 2)])
    normed_low, normed_high = normed_parts(
        pos, query_grad, row_dot, query_weight, 2, [(2, 0), (2, 2)]
    )
    branch_low, branch_high = send_y(branch_low, 1), send_y(branch_high, -1)
    normed_low, normed_high = send_z(normed_low, 1), send_z(normed_high, -1)
    branch_up, branch_down = branch_parts(pos, attended, out_weight, 4, [(1, 0), (3, 0)])
    normed_up, normed_down = normed_parts(
        pos, query_grad, row_dot, query_weight, 4, [(1, 0), (3, 0)]
    )
    out_given = out_weight_terms(pos, attended, all_grads, True)
    branch_up = jnp.concatenate([add(branch_up[:2], branch_low).astype(BF), branch_up[2:]], 0)
    branch_down = jnp.concatenate(
        [branch_down[:2], add(branch_down[2:], branch_high).astype(BF)], 0
    )
    normed_up = jnp.concatenate([add(normed_up[:2], normed_low).astype(BF), normed_up[2:]], 0)
    normed_down = jnp.concatenate(
        [normed_down[:2], add(normed_down[2:], normed_high).astype(BF)], 0
    )
    branch_up, branch_down, normed_up, normed_down = hold(
        branch_up, branch_down, normed_up, normed_down
    )
    branch_up, branch_down = send_y(branch_up, 1), send_y(branch_down, -1)
    normed_up, normed_down = send_z(normed_up, 1), send_z(normed_down, -1)
    branch_own = branch_parts(pos, attended, out_weight, 4, [(0, 0)])[0]
    normed_own = normed_parts(pos, query_grad, row_dot, query_weight, 4, [(0, 0)])[0]

    def over_x(kept, arrived):
        block = [add(kept[k], arrived[k]).astype(BF) for k in range(SIDE)]
        arrived = [send_x(block[1], 1), send_x(block[3], -1), send_x(block[2], 2)]
        return add(block[0], *arrived).astype(BF)

    out_kept = out_weight_terms(pos, attended, all_grads, False)
    out_weight_grad = over_x(out_kept, send_core(out_given))
    query_given = query_weight_terms(pos, query_grad, inverse, small, all_text, True)
    query_kept = query_weight_terms(pos, query_grad, inverse, small, all_text, False)
    query_weight_grad = over_x(query_kept, send_core(query_given))

    near = add(pair_kept, send_core(pair_given)).astype(BF)
    arrived = [near]
    for d, by in ((1, -1), (2, 2), (3, 1)):
        arrived.append(jnp.roll(send_x(near, by), d, axis=0))
    near = add(*arrived).astype(BF)
    far = send_core(near)
    key_weight_grad, value_weight_grad = latent_terms(pos, all_grads, near, far)

    def second(own, up, down, send):
        block = [add(own[k], up[k], down[k]) for k in range(SIDE)]
        sent = [value.astype(BF) for value in block]
        return add(block[0], send(sent[2], 2), send(sent[1], 1), send(sent[3], -1))

    branch = second(branch_own, branch_up, branch_down, send_z)
    normed_sum = second(normed_own, normed_up, normed_down, send_y)
    layer_out = (tanh_gate * branch).astype(BF)
    gate_part = jnp.sum(upstream * branch, axis=0) * (1.0 - tanh_gate * tanh_gate)

    normed_grad, row_sum = normed_sum[:ROWS], normed_sum[ROWS, :ROWS]
    inverse = inverse[:, :1]
    own_unit = text_hidden.astype(F32) * inverse
    unit_grad = normed_grad * norm_gain.astype(F32)
    text_grad = ((unit_grad - own_unit * (row_sum / D)[:, None]) * inverse).astype(BF)
    gain_part = jnp.sum(normed_grad * own_unit, axis=0)
    sums = jnp.stack([gain_part, gate_part])
    sums = sums + send_core(sums)
    sums = sums + send_x(sums, 1) + send_x(sums, -1) + send_x(sums, 2)
    return (
        layer_out,
        text_grad,
        query_weight_grad,
        key_weight_grad,
        value_weight_grad,
        out_weight_grad,
        sums[0],
        sums[1],
    )


def solution(mesh):
    placed = (
        P("dp", "tensor"),
        P("tensor"),
        P("tensor"),
        P("dp", None, "tensor"),
        P(None, "tensor"),
        P(None, "tensor"),
        P(None, "tensor"),
        P("tensor", None),
        P("dp", None),
        P(),
        P("dp", "tensor"),
    )
    return jax.shard_map(
        shards,
        mesh=mesh,
        in_specs=placed,
        out_specs=(
            P("dp", "tensor"),
            P("dp", "tensor"),
            P("dp", "tensor"),
            P("dp", "tensor"),
            P("dp", "tensor"),
            P("tensor", "dp"),
            P("tensor"),
            P("tensor"),
        ),
        check_vma=False,
    )
```

profile of v0, /device:TPU:0, one launch (start us, length us, event | category | flops | bytes accessed | tf_op | source)
XLA Modules:
  0.0 307.6 jit_solution(5335436841270470126)
XLA Ops:
  4.3 3.6 %collective-permute-start.1 = (bf16[80,512]{1,0:T(8,128)(2,1)S(1)}, bf16[80,512]{1,0:T(8,128)(2,1)S(1)}, u32[]{:S(2)}, u32[]{:S(2)}) collective-permute-start(bf16[80,512]{1,0:T(8,128)(2,1)S(1)} %get-tuple-element.101), channel_id=1, source_target_pairs={{0,2},{1,3},{2,0},{3,1},{4,6},{5,7},{6,4},{7,5},{8,10},{9,11},{10,... | collective-permute-start | bytes 245768 | tf_op jit(solution)/shard_map/ppermute | solution.py:32
  14.5 3.2 %collective-permute-start.4 = (bf16[256,512]{1,0:T(8,128)(2,1)}, bf16[256,512]{1,0:T(8,128)(2,1)S(1)}, u32[]{:S(2)}, u32[]{:S(2)}) collective-permute-start(bf16[256,512]{1,0:T(8,128)(2,1)} %param.11), channel_id=1, source_target_pairs={{0,2},{1,3},{2,0},{3,1},{4,6},{5,7},{6,4},{7,5},{8,10},{9,11},{10,... | collective-permute-start | bytes 786440 | tf_op jit(solution)/shard_map/ppermute | solution.py:32
  21.5 6.1 %collective-permute-start.8 = (bf16[320,512]{1,0:T(8,128)(2,1)S(1)}, bf16[320,512]{1,0:T(8,128)(2,1)S(1)}, u32[]{:S(2)}, u32[]{:S(2)}) collective-permute-start(bf16[320,512]{1,0:T(8,128)(2,1)S(1)} %get-tuple-element.97), channel_id=1, source_target_pairs={{0,8},{1,9},{2,10},{3,11},{4,12},{5,13},{6,14},{7,15},{8,0},{9,1},... | collective-permute-start | bytes 983048 | tf_op jit(solution)/shard_map/ppermute | solution.py:37
  34.2 8.2 %collective-permute-done.8 = bf16[320,512]{1,0:T(8,128)(2,1)S(1)} collective-permute-done((bf16[320,512]{1,0:T(8,128)(2,1)S(1)}, bf16[320,512]{1,0:T(8,128)(2,1)S(1)}, u32[]{:S(2)}, u32[]{:S(2)}) %collective-permute-start.8) | collective-permute-done | bytes 327712 | tf_op jit(solution)/shard_map/ppermute | solution.py:37
  50.6 12.3 %collective-permute-done.14 = bf16[4,80,512]{2,1,0:T(8,128)(2,1)S(1)} collective-permute-done((bf16[4,80,512]{2,1,0:T(8,128)(2,1)S(1)}, bf16[4,80,512]{2,1,0:T(8,128)(2,1)S(1)}, u32[]{:S(2)}, u32[]{:S(2)}) %collective-permute-start.14) | collective-permute-done | bytes 327712 | tf_op jit(solution)/shard_map/ppermute | solution.py:37
  65.4 22.3 %collective-permute-done.16 = bf16[4,80,512]{2,1,0:T(8,128)(2,1)S(1)} collective-permute-done((bf16[4,80,512]{2,1,0:T(8,128)(2,1)S(1)}, bf16[4,80,512]{2,1,0:T(8,128)(2,1)S(1)}, u32[]{:S(2)}, u32[]{:S(2)}) %collective-permute-start.16) | collective-permute-done | bytes 327712 | tf_op jit(solution)/shard_map/ppermute | solution.py:37
  96.3 3.7 %shard_map.172.refs_4_ = f32[256,256]{1,0:T(8,128)S(1)} custom-call(s32[4]{0:T(128)S(1)} %pad_add_fusion.pos, bf16[4,320,512]{2,1,0:T(8,128)(2,1)} %pad_maximum_fusion.refs_0_, bf16[256,8192]{1,0:T(8,128)(2,1)S(1)} %copy-done.2), custom_call_target="tpu_custom_call" | custom-call | flops 268435456 | bytes 2097152 | tf_op jit(solution)/shard_map/pallas_call | solution.py:80
  100.0 3.3 %shard_map.171 = (f32[256,256]{1,0:T(8,128)S(1)}, f32[256,128]{1,0:T(8,128)S(1)}) custom-call(s32[4]{0:T(128)S(1)} %pad_add_fusion.pos, bf16[4,256,512]{2,1,0:T(8,128)(2,1)} %pad_maximum_fusion.3.refs_0_, bf16[16,80,512]{2,1,0:T(8,128)(2,1)S(1)} %constant_dynamic-update-slice_fusion.small.refs_1_.refs_2_.refs_3_.gain, bf16[8192,256]{1,0:T(8,128)(2,1)S(1)} %copy-done.3), custom_call_target="tpu_custom_call" | custom-call | flops 268435456 | bytes 2097152 | tf_op jit(solution)/shard_map/pallas_call | solution.py:80
  119.8 3.8 %shard_map.175.refs_4_ = f32[256,256]{1,0:T(8,128)S(1)} custom-call(s32[4]{0:T(128)S(1)} %pad_add_fusion.pos, bf16[4,320,512]{2,1,0:T(8,128)(2,1)} %collective-permute-done.10.refs_0_, bf16[4,320,512]{2,1,0:T(8,128)(2,1)} %collective-permute-done.11.refs_1_, bf16[256,8192]{1,0:T(8,128)(2,1)S(1)} %copy-done.2, bf16[256,8192]{1,0:T(8,128)(2,1)S(1)} %copy-done.2, ...), custom_call_target="tpu_custom_call" | custom-call | flops 536870912 | bytes 4194304 | tf_op jit(solution)/shard_map/pallas_call | solution.py:80
  126.9 4.7 %collective-permute-start.23 = (bf16[2,64,512]{2,1,0:T(8,128)(2,1)S(1)}, bf16[2,64,512]{2,1,0:T(8,128)(2,1)S(1)}, u32[]{:S(2)}, u32[]{:S(2)}) collective-permute-start(bf16[2,64,512]{2,1,0:T(8,128)(2,1)S(1)} %pad_maximum_fusion.9), channel_id=1, source_target_pairs={{0,64},{16,80},{32,96},{48,112},{64,0},{80,16},{96,32},{112,48},{1... | collective-permute-start | bytes 393224 | tf_op jit(solution)/shard_map/ppermute | solution.py:42
  137.3 3.7 %collective-permute-done.22 = bf16[2,64,512]{2,1,0:T(8,128)(2,1)S(1)} collective-permute-done((bf16[2,64,512]{2,1,0:T(8,128)(2,1)S(1)}, bf16[2,64,512]{2,1,0:T(8,128)(2,1)S(1)}, u32[]{:S(2)}, u32[]{:S(2)}) %collective-permute-start.22) | collective-permute-done | bytes 131104 | tf_op jit(solution)/shard_map/ppermute | solution.py:42
  157.9 3.1 %collective-permute-start.26 = (bf16[2,256,512]{2,1,0:T(8,128)(2,1)S(1)}, bf16[2,256,512]{2,1,0:T(8,128)(2,1)}, u32[]{:S(2)}, u32[]{:S(2)}) collective-permute-start(bf16[2,256,512]{2,1,0:T(8,128)(2,1)S(1)} %get-tuple-element.64), channel_id=1, source_target_pairs={{0,12},{1,13},{2,14},{3,15},{4,0},{5,1},{6,2},{7,3},{8,4},{9,5},{1... | collective-permute-start | bytes 1572872 | tf_op jit(solution)/shard_map/ppermute | solution.py:37
  165.2 3.2 %collective-permute-start.28 = (bf16[2,272,512]{2,1,0:T(8,128)(2,1)S(1)}, bf16[2,272,512]{2,1,0:T(8,128)(2,1)S(1)}, u32[]{:S(2)}, u32[]{:S(2)}) collective-permute-start(bf16[2,272,512]{2,1,0:T(8,128)(2,1)S(1)} %get-tuple-element.70), channel_id=1, source_target_pairs={{0,3},{1,0},{2,1},{3,2},{4,7},{5,4},{6,5},{7,6},{8,11},{9,8},{10,9... | collective-permute-start | bytes 1671176 | tf_op jit(solution)/shard_map/ppermute | solution.py:32
  176.3 4.9 %collective-permute-done.27 = bf16[2,272,512]{2,1,0:T(8,128)(2,1)S(1)} collective-permute-done((bf16[2,272,512]{2,1,0:T(8,128)(2,1)S(1)}, bf16[2,272,512]{2,1,0:T(8,128)(2,1)S(1)}, u32[]{:S(2)}, u32[]{:S(2)}) %collective-permute-start.27) | collective-permute-done | bytes 557088 | tf_op jit(solution)/shard_map/ppermute | solution.py:32
  191.2 3.0 shard_map.185
  195.4 3.0 shard_map.184
  203.3 3.1 collective-permute-done.46
  226.5 7.9 %collective-permute-done.33 = bf16[256,512]{1,0:T(8,128)(2,1)S(1)} collective-permute-done((bf16[256,512]{1,0:T(8,128)(2,1)S(1)}, bf16[256,512]{1,0:T(8,128)(2,1)S(1)}, u32[]{:S(2)}, u32[]{:S(2)}) %collective-permute-start.33) | collective-permute-done | bytes 262176 | tf_op jit(solution)/shard_map/ppermute | solution.py:32
  238.0 3.0 collective-permute-start.36
  243.1 3.1 %collective-permute-done.38 = bf16[272,512]{1,0:T(8,128)(2,1)S(1)} collective-permute-done((bf16[272,512]{1,0:T(8,128)(2,1)S(1)}, bf16[272,512]{1,0:T(8,128)(2,1)S(1)}, u32[]{:S(2)}, u32[]{:S(2)}) %collective-permute-start.38) | collective-permute-done | bytes 278560 | tf_op jit(solution)/shard_map/ppermute | solution.py:37
  269.2 5.3 %collective-permute-done.42 = bf16[1024,256]{1,0:T(8,128)(2,1)S(1)} collective-permute-done((bf16[1024,256]{1,0:T(8,128)(2,1)S(1)}, bf16[1024,256]{1,0:T(8,128)(2,1)S(1)}, u32[]{:S(2)}, u32[]{:S(2)}) %collective-permute-start.42) | collective-permute-done | bytes 524320 | tf_op jit(solution)/shard_map/ppermute | solution.py:42
  275.9 9.5 %collective-permute-done.41 = bf16[1024,256]{1,0:T(8,128)(2,1)S(1)} collective-permute-done((bf16[1024,256]{1,0:T(8,128)(2,1)S(1)}, bf16[1024,256]{1,0:T(8,128)(2,1)S(1)}, u32[]{:S(2)}, u32[]{:S(2)}) %collective-permute-start.41) | collective-permute-done | bytes 524320 | tf_op jit(solution)/shard_map/ppermute | solution.py:42
  286.9 10.1 %collective-permute-done.51 = bf16[256,1024]{1,0:T(8,128)(2,1)S(1)} collective-permute-done((bf16[256,1024]{1,0:T(8,128)(2,1)S(1)}, bf16[256,1024]{1,0:T(8,128)(2,1)S(1)}, u32[]{:S(2)}, u32[]{:S(2)}) %collective-permute-start.51) | collective-permute-done | bytes 524320 | tf_op jit(solution)/shard_map/ppermute | solution.py:42
  297.0 9.1 %collective-permute-done.50 = bf16[256,1024]{1,0:T(8,128)(2,1)S(1)} collective-permute-done((bf16[256,1024]{1,0:T(8,128)(2,1)S(1)}, bf16[256,1024]{1,0:T(8,128)(2,1)S(1)}, u32[]{:S(2)}, u32[]{:S(2)}) %collective-permute-start.50) | collective-permute-done | bytes 524320 | tf_op jit(solution)/shard_map/ppermute | solution.py:42
  (226 shorter events, 163.0 us)
Async XLA Ops:
  21.5 20.9 %collective-permute-start.8 = (bf16[320,512]{1,0:T(8,128)(2,1)S(1)}, bf16[320,512]{1,0:T(8,128)(2,1)S(1)}, u32[]{:S(2)}, u32[]{:S(2)}) collective-permute-start(bf16[320,512]{1,0:T(8,128)(2,1)S(1)} %get-tuple-element.97), channel_id=1, source_target_pairs={{0,8},{1,9},{2,10},{3,11},{4,12},{5,13},{6,14},{7,15},{8,0},{9,1},... | collective-permute-start | bytes 983048 | tf_op jit(solution)/shard_map/ppermute | solution.py:37
  43.6 59.7 %collective-permute-start.10 = (bf16[4,320,512]{2,1,0:T(8,128)(2,1)}, bf16[4,320,512]{2,1,0:T(8,128)(2,1)}, u32[]{:S(2)}, u32[]{:S(2)}) collective-permute-start(bf16[4,320,512]{2,1,0:T(8,128)(2,1)} %pad_maximum_fusion.refs_0_), channel_id=1, source_target_pairs={{0,3},{1,0},{2,1},{3,2},{4,7},{5,4},{6,5},{7,6},{8,11},{9,8},{10,9... | collective-permute-start | bytes 3932168 | tf_op jit(solution)/shard_map/ppermute | solution.py:32
  44.2 59.2 %collective-permute-start.11 = (bf16[4,320,512]{2,1,0:T(8,128)(2,1)}, bf16[4,320,512]{2,1,0:T(8,128)(2,1)}, u32[]{:S(2)}, u32[]{:S(2)}) collective-permute-start(bf16[4,320,512]{2,1,0:T(8,128)(2,1)} %pad_maximum_fusion.refs_0_), channel_id=1, source_target_pairs={{0,1},{1,2},{2,3},{3,0},{4,5},{5,6},{6,7},{7,4},{8,9},{9,10},{10,1... | collective-permute-start | bytes 3932168 | tf_op jit(solution)/shard_map/ppermute | solution.py:32
  49.8 53.5 %collective-permute-start.12 = (bf16[4,256,512]{2,1,0:T(8,128)(2,1)}, bf16[4,256,512]{2,1,0:T(8,128)(2,1)S(1)}, u32[]{:S(2)}, u32[]{:S(2)}) collective-permute-start(bf16[4,256,512]{2,1,0:T(8,128)(2,1)} %pad_maximum_fusion.3.refs_0_), channel_id=1, source_target_pairs={{0,12},{1,13},{2,14},{3,15},{4,0},{5,1},{6,2},{7,3},{8,4},{9,5},{1... | collective-permute-start | bytes 3145736 | tf_op jit(solution)/shard_map/ppermute | solution.py:37
  62.9 40.4 %collective-permute-start.13 = (bf16[4,256,512]{2,1,0:T(8,128)(2,1)}, bf16[4,256,512]{2,1,0:T(8,128)(2,1)S(1)}, u32[]{:S(2)}, u32[]{:S(2)}) collective-permute-start(bf16[4,256,512]{2,1,0:T(8,128)(2,1)} %pad_maximum_fusion.3.refs_0_), channel_id=1, source_target_pairs={{0,4},{1,5},{2,6},{3,7},{4,8},{5,9},{6,10},{7,11},{8,12},{9,13},{1... | collective-permute-start | bytes 3145736 | tf_op jit(solution)/shard_map/ppermute | solution.py:37
  65.2 22.6 %collective-permute-start.16 = (bf16[4,80,512]{2,1,0:T(8,128)(2,1)S(1)}, bf16[4,80,512]{2,1,0:T(8,128)(2,1)S(1)}, u32[]{:S(2)}, u32[]{:S(2)}) collective-permute-start(bf16[4,80,512]{2,1,0:T(8,128)(2,1)S(1)} %pad_maximum_fusion.7), channel_id=1, source_target_pairs={{0,4},{1,5},{2,6},{3,7},{4,8},{5,9},{6,10},{7,11},{8,12},{9,13},{1... | collective-permute-start | bytes 983048 | tf_op jit(solution)/shard_map/ppermute | solution.py:37
  104.3 37.7 %collective-permute-start.18 = (bf16[2,256,512]{2,1,0:T(8,128)(2,1)}, bf16[2,256,512]{2,1,0:T(8,128)(2,1)}, u32[]{:S(2)}, u32[]{:S(2)}) collective-permute-start(bf16[2,256,512]{2,1,0:T(8,128)(2,1)} %slice.195), channel_id=1, source_target_pairs={{0,4},{1,5},{2,6},{3,7},{4,8},{5,9},{6,10},{7,11},{8,12},{9,13},{1... | collective-permute-start | bytes 1572872 | tf_op jit(solution)/shard_map/ppermute | solution.py:37
  106.2 35.7 %collective-permute-start.19 = (bf16[2,256,512]{2,1,0:T(8,128)(2,1)}, bf16[2,256,512]{2,1,0:T(8,128)(2,1)}, u32[]{:S(2)}, u32[]{:S(2)}) collective-permute-start(bf16[2,256,512]{2,1,0:T(8,128)(2,1)} %slice.196), channel_id=1, source_target_pairs={{0,12},{1,13},{2,14},{3,15},{4,0},{5,1},{6,2},{7,3},{8,4},{9,5},{1... | collective-permute-start | bytes 1572872 | tf_op jit(solution)/shard_map/ppermute | solution.py:37
  110.4 34.1 %collective-permute-start.20 = (bf16[2,320,512]{2,1,0:T(8,128)(2,1)}, bf16[2,320,512]{2,1,0:T(8,128)(2,1)S(1)}, u32[]{:S(2)}, u32[]{:S(2)}) collective-permute-start(bf16[2,320,512]{2,1,0:T(8,128)(2,1)} %slice.197), channel_id=1, source_target_pairs={{0,1},{1,2},{2,3},{3,0},{4,5},{5,6},{6,7},{7,4},{8,9},{9,10},{10,1... | collective-permute-start | bytes 1966088 | tf_op jit(solution)/shard_map/ppermute | solution.py:32
  112.8 31.7 %collective-permute-start.21 = (bf16[2,320,512]{2,1,0:T(8,128)(2,1)}, bf16[2,320,512]{2,1,0:T(8,128)(2,1)}, u32[]{:S(2)}, u32[]{:S(2)}) collective-permute-start(bf16[2,320,512]{2,1,0:T(8,128)(2,1)} %slice.198), channel_id=1, source_target_pairs={{0,3},{1,0},{2,1},{3,2},{4,7},{5,4},{6,5},{7,6},{8,11},{9,8},{10,9... | collective-permute-start | bytes 1966088 | tf_op jit(solution)/shard_map/ppermute | solution.py:32
  151.0 20.6 %collective-permute-start.25 = (bf16[2,256,512]{2,1,0:T(8,128)(2,1)S(1)}, bf16[2,256,512]{2,1,0:T(8,128)(2,1)}, u32[]{:S(2)}, u32[]{:S(2)}) collective-permute-start(bf16[2,256,512]{2,1,0:T(8,128)(2,1)S(1)} %get-tuple-element.62), channel_id=1, source_target_pairs={{0,4},{1,5},{2,6},{3,7},{4,8},{5,9},{6,10},{7,11},{8,12},{9,13},{1... | collective-permute-start | bytes 1572872 | tf_op jit(solution)/shard_map/ppermute | solution.py:37
  151.1 17.3 %collective-permute-start.43 = (bf16[4,64,512]{2,1,0:T(8,128)(2,1)S(1)}, bf16[4,64,512]{2,1,0:T(8,128)(2,1)S(1)}, u32[]{:S(2)}, u32[]{:S(2)}) collective-permute-start(bf16[4,64,512]{2,1,0:T(8,128)(2,1)S(1)} %get-tuple-element.77), channel_id=1, source_target_pairs={{0,16},{16,0},{32,48},{48,32},{64,80},{80,64},{96,112},{112,96},{1... | collective-permute-start | bytes 786440 | tf_op jit(solution)/shard_map/ppermute | solution.py:46
  169.2 29.2 %collective-permute-start.44 = (bf16[4,64,512]{2,1,0:T(8,128)(2,1)}, bf16[4,64,512]{2,1,0:T(8,128)(2,1)}, u32[]{:S(2)}, u32[]{:S(2)}) collective-permute-start(bf16[4,64,512]{2,1,0:T(8,128)(2,1)} %add_convert_fusion.16), channel_id=1, source_target_pairs={{0,96},{16,112},{32,0},{48,16},{64,32},{80,48},{96,64},{112,80},{1... | collective-permute-start | bytes 786440 | tf_op jit(solution)/shard_map/ppermute | solution.py:42
  183.7 34.3 %collective-permute-start.30 = (bf16[4,256,512]{2,1,0:T(8,128)(2,1)}, bf16[4,256,512]{2,1,0:T(8,128)(2,1)}, u32[]{:S(2)}, u32[]{:S(2)}) collective-permute-start(bf16[4,256,512]{2,1,0:T(8,128)(2,1)} %pad_maximum_fusion.5), channel_id=1, source_target_pairs={{0,12},{1,13},{2,14},{3,15},{4,0},{5,1},{6,2},{7,3},{8,4},{9,5},{1... | collective-permute-start | bytes 3145736 | tf_op jit(solution)/shard_map/ppermute | solution.py:37
  184.0 34.6 %collective-permute-start.29 = (bf16[4,256,512]{2,1,0:T(8,128)(2,1)}, bf16[4,256,512]{2,1,0:T(8,128)(2,1)}, u32[]{:S(2)}, u32[]{:S(2)}) collective-permute-start(bf16[4,256,512]{2,1,0:T(8,128)(2,1)} %pad_maximum_fusion.4), channel_id=1, source_target_pairs={{0,4},{1,5},{2,6},{3,7},{4,8},{5,9},{6,10},{7,11},{8,12},{9,13},{1... | collective-permute-start | bytes 3145736 | tf_op jit(solution)/shard_map/ppermute | solution.py:37
  186.9 36.0 %collective-permute-start.35 = (bf16[4,272,512]{2,1,0:T(8,128)(2,1)}, bf16[4,272,512]{2,1,0:T(8,128)(2,1)}, u32[]{:S(2)}, u32[]{:S(2)}) collective-permute-start(bf16[4,272,512]{2,1,0:T(8,128)(2,1)} %pad_maximum_fusion.2), channel_id=1, source_target_pairs={{0,3},{1,0},{2,1},{3,2},{4,7},{5,4},{6,5},{7,6},{8,11},{9,8},{10,9... | collective-permute-start | bytes 3342344 | tf_op jit(solution)/shard_map/ppermute | solution.py:32
  188.6 34.3 %collective-permute-start.34 = (bf16[4,272,512]{2,1,0:T(8,128)(2,1)}, bf16[4,272,512]{2,1,0:T(8,128)(2,1)}, u32[]{:S(2)}, u32[]{:S(2)}) collective-permute-start(bf16[4,272,512]{2,1,0:T(8,128)(2,1)} %pad_maximum_fusion.1), channel_id=1, source_target_pairs={{0,1},{1,2},{2,3},{3,0},{4,5},{5,6},{6,7},{7,4},{8,9},{9,10},{10,1... | collective-permute-start | bytes 3342344 | tf_op jit(solution)/shard_map/ppermute | solution.py:32
  217.9 38.8 %collective-permute-start.39 = (bf16[4,1024,256]{2,1,0:T(8,128)(2,1)S(1)}, bf16[4,1024,256]{2,1,0:T(8,128)(2,1)S(1)}, u32[]{:S(2)}, u32[]{:S(2)}) collective-permute-start(bf16[4,1024,256]{2,1,0:T(8,128)(2,1)S(1)} %copy-done.13), channel_id=1, source_target_pairs={{0,16},{16,0},{32,48},{48,32},{64,80},{80,64},{96,112},{112,96},{1... | collective-permute-start | bytes 6291464 | tf_op jit(solution)/shard_map/ppermute | solution.py:46
  218.1 45.8 %collective-permute-start.48 = (bf16[4,256,1024]{2,1,0:T(8,128)(2,1)S(1)}, bf16[4,256,1024]{2,1,0:T(8,128)(2,1)S(1)}, u32[]{:S(2)}, u32[]{:S(2)}) collective-permute-start(bf16[4,256,1024]{2,1,0:T(8,128)(2,1)S(1)} %shard_map.188), channel_id=1, source_target_pairs={{0,16},{16,0},{32,48},{48,32},{64,80},{80,64},{96,112},{112,96},{1... | collective-permute-start | bytes 6291464 | tf_op jit(solution)/shard_map/ppermute | solution.py:46
  261.3 24.1 %collective-permute-start.41 = (bf16[1024,256]{1,0:T(8,128)(2,1)S(1)}, bf16[1024,256]{1,0:T(8,128)(2,1)S(1)}, u32[]{:S(2)}, u32[]{:S(2)}) collective-permute-start(bf16[1024,256]{1,0:T(8,128)(2,1)S(1)} %get-tuple-element.85), channel_id=1, source_target_pairs={{0,96},{16,112},{32,0},{48,16},{64,32},{80,48},{96,64},{112,80},{1... | collective-permute-start | bytes 1572872 | tf_op jit(solution)/shard_map/ppermute | solution.py:42
  263.9 21.9 %collective-permute-start.40 = (bf16[1024,256]{1,0:T(8,128)(2,1)S(1)}, bf16[1024,256]{1,0:T(8,128)(2,1)S(1)}, u32[]{:S(2)}, u32[]{:S(2)}) collective-permute-start(bf16[1024,256]{1,0:T(8,128)(2,1)S(1)} %get-tuple-element.83), channel_id=1, source_target_pairs={{0,32},{16,48},{32,64},{48,80},{64,96},{80,112},{96,0},{112,16},{1... | collective-permute-start | bytes 1572872 | tf_op jit(solution)/shard_map/ppermute | solution.py:42
  264.6 32.4 %collective-permute-start.51 = (bf16[256,1024]{1,0:T(8,128)(2,1)S(1)}, bf16[256,1024]{1,0:T(8,128)(2,1)S(1)}, u32[]{:S(2)}, u32[]{:S(2)}) collective-permute-start(bf16[256,1024]{1,0:T(8,128)(2,1)S(1)} %get-tuple-element.81), channel_id=1, source_target_pairs={{0,64},{16,80},{32,96},{48,112},{64,0},{80,16},{96,32},{112,48},{1... | collective-permute-start | bytes 1572872 | tf_op jit(solution)/shard_map/ppermute | solution.py:42
  266.8 39.3 %collective-permute-start.50 = (bf16[256,1024]{1,0:T(8,128)(2,1)S(1)}, bf16[256,1024]{1,0:T(8,128)(2,1)S(1)}, u32[]{:S(2)}, u32[]{:S(2)}) collective-permute-start(bf16[256,1024]{1,0:T(8,128)(2,1)S(1)} %get-tuple-element.82), channel_id=1, source_target_pairs={{0,96},{16,112},{32,0},{48,16},{64,32},{80,48},{96,64},{112,80},{1... | collective-permute-start | bytes 1572872 | tf_op jit(solution)/shard_map/ppermute | solution.py:42
  274.5 31.9 %collective-permute-start.49 = (bf16[256,1024]{1,0:T(8,128)(2,1)S(1)}, bf16[256,1024]{1,0:T(8,128)(2,1)S(1)}, u32[]{:S(2)}, u32[]{:S(2)}) collective-permute-start(bf16[256,1024]{1,0:T(8,128)(2,1)S(1)} %get-tuple-element.80), channel_id=1, source_target_pairs={{0,32},{16,48},{32,64},{48,80},{64,96},{80,112},{96,0},{112,16},{1... | collective-permute-start | bytes 1572872 | tf_op jit(solution)/shard_map/ppermute | solution.py:42
  (56 other events, 572.3 us)
where the time goes:
time: 310 us; the launch traced here: 308 us
  waiting for transfers between devices  110 us (35%)
  starting transfers between devices  89.9 us (29%)
  Pallas kernels  46.7 us (15%)
  local copies, waits for them, and re-layouts  33.2 us (11%)
  other arithmetic  26.8 us (9%)
    ppermute x17, waiting for transfers between devices, send_y(): return lax.ppermute(value, 'tensor', pairs)  51.2 us
    pallas_call x19, Pallas kernels, call(): pl.pallas_call(body, grid_spec=pltpu.PrefetchScalarGridSpec(num_scalar_pr...  46.7 us
    ppermute x15, waiting for transfers between devices, send_x(): lax.ppermute(value, 'dp', [(i, (i + by * CORES) % count) for i in range(c...  43.1 us
    ppermute x17, starting transfers between devices, send_y(): return lax.ppermute(value, 'tensor', pairs)  30.7 us
    ppermute x15, starting transfers between devices, send_x(): lax.ppermute(value, 'dp', [(i, (i + by * CORES) % count) for i in range(c...  29.3 us
    ppermute x17, starting transfers between devices, send_z(): return lax.ppermute(value, 'tensor', pairs)  26.9 us
    unnamed x55, local copies, waits for them, and re-layouts  18.4 us
    ppermute x17, waiting for transfers between devices, send_z(): return lax.ppermute(value, 'tensor', pairs)  15.3 us
  transfers between devices with their start and end apart: 56, of which 20 were waited for; matrix products, arithmetic and copies ran while one was open for 15% of the time, Pallas kernels for 13%

commit v1 on v0

v1 whole, which is shorter than its diff:
```python
import functools

import jax
import jax.numpy as jnp
from jax import lax
from jax.experimental import pallas as pl
from jax.experimental.pallas import tpu as pltpu
from jax.sharding import PartitionSpec as P

D = 8192
HEAD_DIM = 128
SIDE = 4
CORES = 2
LAT = 64
ROWS = 256
WIDTH = 512
COLS = 256
EXTRA = 16
EPSILON = 1e-05
COST = 64
SCALE = HEAD_DIM ** (-0.5)

BF = jnp.bfloat16
F32 = jnp.float32


def dot(left, right, over):
    return lax.dot_general(left, right, ((over[:1], over[1:]), ((), ())), preferred_element_type=F32)


def ring_send(value, by, axis):
    moves = []
    for x in range(SIDE):
        for core in range(CORES):
            for y in range(SIDE):
                for z in range(SIDE):
                    to = {"x": x, "y": y, "z": z}
                    to[axis] = (to[axis] + (by if core == 0 else -by)) % SIDE
                    source = ((x * CORES + core) * SIDE + y) * SIDE + z
                    target = ((to["x"] * CORES + core) * SIDE + to["y"]) * SIDE + to["z"]
                    moves.append((source, target))
    return lax.ppermute(value, ("dp", "tensor"), moves)


send_x = functools.partial(ring_send, axis="x")
send_y = functools.partial(ring_send, axis="y")
send_z = functools.partial(ring_send, axis="z")


def send_core(value):
    return lax.ppermute(value, "dp", [(i, i ^ 1) for i in range(SIDE * CORES)])


def hold(*values):
    return lax.optimization_barrier(values)


def gather_direct(value, send):
    across, above, below = send(value, 2), send(value, -1), send(value, 1)
    return [value, above, across, below]


def gather_ring(value, send):
    below, above = send(value, 1), send(value, -1)
    return [value, above, send(below, 1), below]


def add(*terms):
    total = terms[0].astype(F32)
    for term in terms[1:]:
        total = total + term.astype(F32)
    return total


def ahead(pos, axis, distance):
    return lax.rem(pos[axis] + (1 - 2 * pos[1]) * distance + SIDE, SIDE)


def distance_to(pos, axis, place):
    return lax.rem((1 - 2 * pos[1]) * (place - pos[axis]) + SIDE, SIDE)


def feature_block(pos, ky, kz):
    return ahead(pos, 2, ky) * SIDE + ahead(pos, 3, kz)


def call(body, pos, grid, ins, outs, scratch, flops, moved, aliases=None):
    arrays, in_specs = zip(*ins)
    shapes, out_specs = zip(*outs)
    return pl.pallas_call(
        body,
        grid_spec=pltpu.PrefetchScalarGridSpec(
            num_scalar_prefetch=1,
            grid=grid,
            in_specs=list(in_specs),
            out_specs=list(out_specs),
            scratch_shapes=scratch,
        ),
        out_shape=list(shapes),
        compiler_params=pltpu.CompilerParams(
            dimension_semantics=("arbitrary",) * len(grid), vmem_limit_bytes=24 * 2**20
        ),
        input_output_aliases=aliases or {},
        cost_estimate=pl.CostEstimate(flops=flops // COST, bytes_accessed=moved // COST, transcendentals=0),
    )(pos, *arrays)


def whole(array):
    zeros = (0,) * array.ndim
    return array, pl.BlockSpec(array.shape, lambda *_: zeros)


def whole_out(shape, dtype):
    zeros = (0,) * len(shape)
    return jax.ShapeDtypeStruct(shape, dtype), pl.BlockSpec(shape, lambda *_: zeros)


def query_body(count, first, last, pos, *refs):
    pieces, gains, weights = refs[:count], refs[count : 2 * count], refs[2 * count : 3 * count]
    rest = refs[3 * count :]
    if not first:
        total_in, squares_in, *rest = rest
    out_a, out_b, total, squares = rest
    step = pl.program_id(0)

    @pl.when(step == 0)
    def _():
        if first:
            total[...] = jnp.zeros_like(total)
            squares[...] = jnp.zeros_like(squares)
        else:
            total[...] = total_in[...]
            squares[...] = squares_in[...]

    for piece, gain, weight in zip(pieces, gains, weights):
        text = piece[0].astype(F32)
        square = text * text
        squares[...] += (square[:, :128] + square[:, 128:256]) + (
            square[:, 256:384] + square[:, 384:]
        )
        scaled = (text * gain[0][:1].astype(F32)).astype(BF)
        total[...] += dot(scaled, weight[...], (1, 0))

    @pl.when(step == pl.num_programs(0) - 1)
    def _():
        if last:
            mean = jnp.sum(squares[...], axis=1, keepdims=True) / D
            inverse = lax.rsqrt(mean + EPSILON)
            out_a[...] = (total[...] * inverse).astype(BF)
            out_b[...] = jnp.broadcast_to(inverse, out_b.shape)
        else:
            out_a[...] = total[...]
            out_b[...] = squares[...]


def query_part(pos, arrays, places, gains, weight, carry, last):
    steps = arrays[0].shape[0]
    ins = [(a, pl.BlockSpec((1, ROWS, WIDTH), lambda i, pos: (i, 0, 0))) for a in arrays]
    for array, at, row in gains:
        index = lambda i, pos, at=at, row=row: (at + i, row // EXTRA, 0)
        ins.append((array, pl.BlockSpec((1, EXTRA, WIDTH), index)))
    for ky, kz in places:
        index = lambda i, pos, ky=ky, kz=kz: (feature_block(pos, ky, kz + i), 0)
        ins.append((weight, pl.BlockSpec((WIDTH, COLS), index)))
    ins += [whole(value) for value in carry]
    outs = [
        whole_out((ROWS, COLS), BF if last else F32),
        whole_out((ROWS, 128), F32),
    ]
    scratch = [pltpu.VMEM((ROWS, COLS), F32), pltpu.VMEM((ROWS, 128), F32)]
    body = functools.partial(query_body, len(arrays), not carry, last)
    work = steps * len(arrays)
    return call(body, pos, (steps,), ins, outs, scratch, work * 2 * ROWS * WIDTH * COLS, work * 2**19)


def grad_body(count, first, last, pos, *refs):
    pieces, weights, rest = refs[:count], refs[count : 2 * count], refs[2 * count :]
    if not first:
        total_in, *rest = rest
    out, total = rest
    step = pl.program_id(0)

    @pl.when(step == 0)
    def _():
        total[...] = jnp.zeros_like(total) if first else total_in[...]

    for piece, weight in zip(pieces, weights):
        total[...] += dot(piece[0], weight[...], (1, 1))

    @pl.when(step == pl.num_programs(0) - 1)
    def _():
        out[...] = total[...].astype(out.dtype)


def grad_part(pos, arrays, places, weight, carry, last):
    steps = arrays[0].shape[0]
    ins = [(a, pl.BlockSpec((1, ROWS, WIDTH), lambda i, pos: (i, 0, 0))) for a in arrays]
    for kz, ky in places:
        index = lambda i, pos, ky=ky, kz=kz: (0, feature_block(pos, ky + i, kz))
        ins.append((weight, pl.BlockSpec((COLS, WIDTH), index)))
    ins += [whole(value) for value in carry]
    outs = [whole_out((ROWS, COLS), BF if last else F32)]
    body = functools.partial(grad_body, len(arrays), not carry, last)
    work = steps * len(arrays)
    scratch = [pltpu.VMEM((ROWS, COLS), F32)]
    return call(body, pos, (steps,), ins, outs, scratch, work * 2 * ROWS * WIDTH * COLS, work * 2**19)


def pair_body(pos, *refs):
    latents, keys, values = refs[:SIDE], refs[SIDE : 2 * SIDE], refs[2 * SIDE : 3 * SIDE]
    out, total = refs[-2:]
    step = pl.program_id(0)

    @pl.when(step == 0)
    def _():
        total[...] = jnp.zeros_like(total)

    def body(rows):
        for kz in range(SIDE):
            total[:, :COLS] += dot(rows[kz], keys[kz][...], (1, 0))
            total[:, COLS:] += dot(rows[kz], values[kz][...], (1, 0))

    at_piece(latents, [1] * SIDE, step, body)

    @pl.when(step == SIDE - 1)
    def _():
        out[...] = total[...].astype(BF)


def at_piece(refs, counts, step, body):
    first = 0
    for ref, count in zip(refs, counts):
        pl.when((step >= first) & (step < first + count))(functools.partial(body, ref))
        first += count


def own_pair(pos, arrays, firsts, key_weight, value_weight):
    ins = []
    for array, first in zip(arrays, firsts):
        index = lambda i, pos, first=first: (0, first // LAT, 0)
        ins.append((array, pl.BlockSpec((SIDE, LAT, WIDTH), index)))
    for weight in (key_weight, value_weight):
        for kz in range(SIDE):
            index = lambda i, pos, kz=kz: (feature_block(pos, i, kz), 0)
            ins.append((weight, pl.BlockSpec((WIDTH, COLS), index)))
    outs = [whole_out((LAT, 2 * COLS), BF)]
    scratch = [pltpu.VMEM((LAT, 2 * COLS), F32)]
    return call(pair_body, pos, (SIDE,), ins, outs, scratch, 2 * LAT * D * 512, 10 * 2**20)[0]


def attention_body(
    pos, queries, grads, pair, inverse, attended, query_grad, scaled, kept, given, row_dot, part
):
    part[...] = jnp.zeros_like(part)
    span = ROWS // 2
    ones = jnp.ones((8, COLS), F32)
    for c in range(2):
        rows = slice(c * span, (c + 1) * span)
        places = [pos[4 + c * 4 + j] for j in range(4)]
        blocks = [pair[at] for at in places]
        product, key_grads, value_grads = [], [], []
        for h in range(2):
            cols = slice(h * HEAD_DIM, (h + 1) * HEAD_DIM)
            value_cols = slice(COLS + h * HEAD_DIM, COLS + (h + 1) * HEAD_DIM)
            keys = jnp.concatenate([block[:, cols] for block in blocks], 0)
            values = jnp.concatenate([block[:, value_cols] for block in blocks], 0)
            query, grad = queries[rows, cols], grads[rows, cols]
            scores = dot(query, keys, (1, 1)) * SCALE
            scores = jnp.exp(scores - jnp.max(scores, axis=1, keepdims=True))
            probs = scores / jnp.sum(scores, axis=1, keepdims=True)
            probs_low = probs.astype(BF)
            attended[rows, cols] = dot(probs_low, values, (1, 0)).astype(BF)
            probs_grad = dot(grad, values, (1, 1))
            inner = jnp.sum(probs * probs_grad, axis=1, keepdims=True)
            score_low = (probs * (probs_grad - inner) * SCALE).astype(BF)
            out = dot(score_low, keys, (1, 0)).astype(BF)
            query_grad[rows, cols] = out
            scaled[rows, cols] = (out.astype(F32) * inverse[rows]).astype(BF)
            product.append(out.astype(F32) * query.astype(F32))
            key_grads.append(dot(score_low, query, (0, 0)))
            value_grads.append(dot(probs_low, grad, (0, 0)))
        pair_grad = jnp.concatenate(key_grads + value_grads, 1)
        for j in range(4):
            part[places[j]] += pair_grad[j * LAT : (j + 1) * LAT]
        line = lax.dot_general(
            ones,
            jnp.concatenate(product, 1),
            (((1,), (1,)), ((), ())),
            precision=lax.Precision.HIGHEST,
            preferred_element_type=F32,
        )
        row_dot[:, rows] = jnp.concatenate([line, line], 0).astype(BF)
    row_dot[:, ROWS:] = jnp.zeros((EXTRA, WIDTH - ROWS), BF)
    for kx in range(SIDE):
        kept[kx] = part[ahead(pos, 0, kx) * CORES + pos[1]].astype(BF)
        given[kx] = part[ahead(pos, 0, (SIDE - kx) % SIDE) * CORES + 1 - pos[1]].astype(BF)


def attention(pos_slots, queries, grads, pair, inverse):
    ins = [whole(queries), whole(grads), whole(pair), whole(inverse)]
    outs = [
        whole_out((ROWS, COLS), BF),
        whole_out((ROWS, COLS), BF),
        whole_out((ROWS, COLS), BF),
        whole_out((SIDE, LAT, 2 * COLS), BF),
        whole_out((SIDE, LAT, 2 * COLS), BF),
        whole_out((EXTRA, WIDTH), BF),
    ]
    scratch = [pltpu.VMEM((SIDE * CORES, LAT, 2 * COLS), F32)]
    return call(attention_body, pos_slots, (1,), ins, outs, scratch, 4 * 10 * 2**23, 3 * 2**20)


def parts_body(count, over, pos, left, *refs):
    weights, rest = refs[:count], refs[count:]
    tail = None
    if len(rest) > count:
        tail, *rest = rest
    for weight, out in zip(weights, rest):
        out[0, :ROWS] = dot(left[...], weight[...], over).astype(BF)
        if tail is not None:
            out[0, ROWS:] = tail[...]


def branch_parts(pos, left, weight, steps, places):
    ins = [whole(left)]
    outs = []
    for ky, kz in places:
        index = lambda i, pos, ky=ky, kz=kz: (0, feature_block(pos, ky, kz + i))
        ins.append((weight, pl.BlockSpec((COLS, WIDTH), index)))
        shape = jax.ShapeDtypeStruct((steps, ROWS, WIDTH), BF)
        outs.append((shape, pl.BlockSpec((1, ROWS, WIDTH), lambda i, pos: (i, 0, 0))))
    body = functools.partial(parts_body, len(places), (1, 0))
    work = steps * len(places)
    return call(body, pos, (steps,), ins, outs, [], work * 2 * ROWS * WIDTH * COLS, work * 2**19)


def normed_parts(pos, left, tail, weight, steps, places):
    ins = [whole(left)]
    outs = []
    for kz, ky in places:
        index = lambda i, pos, ky=ky, kz=kz: (feature_block(pos, ky + i, kz), 0)
        ins.append((weight, pl.BlockSpec((WIDTH, COLS), index)))
        shape = jax.ShapeDtypeStruct((steps, ROWS + EXTRA, WIDTH), BF)
        outs.append((shape, pl.BlockSpec((1, ROWS + EXTRA, WIDTH), lambda i, pos: (i, 0, 0))))
    ins.append(whole(tail))
    body = functools.partial(parts_body, len(places), (1, 1))
    work = steps * len(places)
    return call(body, pos, (steps,), ins, outs, [], work * 2 * ROWS * WIDTH * COLS, work * 2**19)


def half_at(place):
    return pl.ds(pl.multiple_of(lax.rem(place, CORES) * WIDTH, WIDTH), WIDTH)


def spread(arrays):
    spec = pl.BlockSpec((1, ROWS, WIDTH), lambda s, pos: (s, 0, 0))
    return [(array, spec) for array in arrays]


def out_weight_body(pos, attended, *refs):
    for kz in range(SIDE):
        place = ahead(pos, 3, kz)
        value = dot(attended[...], refs[kz][0], (0, 0)).astype(BF)
        refs[-1][0, place // CORES, :, half_at(place)] = value


def out_weight_terms(pos, attended, grads):
    shape = jax.ShapeDtypeStruct((SIDE, CORES, COLS, 2 * WIDTH), BF)
    index = lambda s, pos: (ahead(pos, 2, s), 0, 0, 0)
    outs = [(shape, pl.BlockSpec((1, CORES, COLS, 2 * WIDTH), index))]
    ins = [whole(attended)] + spread(grads)
    out = call(out_weight_body, pos, (SIDE,), ins, outs, [], 16 * 2**26, 16 * 2**19)[0]
    return out.reshape(8, COLS, 2 * WIDTH)


def query_weight_body(pos, query_grad, *refs):
    for ky in range(SIDE):
        refs[-1][ahead(pos, 2, ky), 0] = dot(refs[ky][0], query_grad[...], (0, 0)).astype(BF)


def query_weight_terms(pos, query_grad, text):
    def index(s, pos):
        at = ahead(pos, 3, s)
        return 0, at // CORES, lax.rem(at, CORES), 0

    shape = jax.ShapeDtypeStruct((SIDE, CORES, 2 * WIDTH, COLS), BF)
    outs = [(shape, pl.BlockSpec((SIDE, 1, WIDTH, COLS), index))]
    ins = [whole(query_grad)] + spread(text)
    out = call(query_weight_body, pos, (SIDE,), ins, outs, [], 16 * 2**26, 16 * 2**19)[0]
    return out.reshape(8, 2 * WIDTH, COLS)


def add_body(count, pos, *refs):
    sums, terms, outs = refs[:count], refs[count : 2 * count], refs[2 * count :]
    for total, term, out in zip(sums, terms, outs):
        out[...] = (total[...].astype(F32) + term[...].astype(F32)).astype(BF)


def add_arrived(pos, sums, terms):
    ins, outs = [], []
    for total in sums:
        spec = pl.BlockSpec((1,) + total.shape[1:], lambda i, pos: (i, 0, 0))
        ins.append((total, spec))
        outs.append((jax.ShapeDtypeStruct(total.shape, BF), spec))
    for term in terms:
        ins.append((term, pl.BlockSpec((1,) + term.shape[1:], lambda i, pos: (i, 0, 0))))
    body = functools.partial(add_body, len(sums))
    aliases = {1 + i: i for i in range(len(sums))}
    return call(body, pos, (SIDE,), ins, outs, [], 2**20, 6 * 2**20, aliases)


def slice_body(pos, *refs):
    given, kept = refs[-2:]
    for ky in range(SIDE):
        kx = distance_to(pos, 0, ahead(pos, 2, ky))
        for kz in range(SIDE):
            place = ahead(pos, 3, kz)
            cols = half_at(place)
            mine = place // CORES == pos[1]

            @pl.when(mine)
            def _(ky=ky, kz=kz, kx=kx, cols=cols):
                kept[kx, :, cols] = refs[ky][kz]

            @pl.when(jnp.logical_not(mine))
            def _(ky=ky, kz=kz, kx=kx, cols=cols):
                given[lax.rem(SIDE - kx, SIDE), :, cols] = refs[ky][kz]


def latent_slices(pos, small):
    ins = [(a, pl.BlockSpec((SIDE, LAT, WIDTH), lambda i, pos: (0, 0, 0))) for a in small]
    outs = [whole_out((SIDE, LAT, 2 * WIDTH), BF), whole_out((SIDE, LAT, 2 * WIDTH), BF)]
    return call(slice_body, pos, (1,), ins, outs, [], 2**10, 2**21)


def latent_body(pos, *refs):
    slices, (near, far, key_out, value_out) = refs[:SIDE], refs[SIDE:]
    left, right = [], []
    for kx in range(SIDE):
        left += [slices[kx][0], slices[kx][1]]
        right += [near[kx], far[(SIDE - kx) % SIDE]]
    right = jnp.concatenate(right, 0)
    for half in range(2):
        rows = slice(half * WIDTH, (half + 1) * WIDTH)
        block = jnp.concatenate([part[:, rows] for part in left], 0)
        total = dot(block, right, (0, 0)).astype(BF)
        key_out[rows] = total[:, :COLS]
        value_out[rows] = total[:, COLS:]


def latent_terms(pos, slices, near, far):
    ins = [whole(array) for array in slices] + [whole(near), whole(far)]
    outs = [whole_out((2 * WIDTH, COLS), BF), whole_out((2 * WIDTH, COLS), BF)]
    return call(latent_body, pos, (1,), ins, outs, [], 2**30, 3 * 2**20)


def shards(
    text_hidden,
    norm_gain,
    gate_alpha,
    latents,
    query_weight,
    key_weight,
    value_weight,
    out_weight,
    citations,
    image_slot,
    out_grad,
):
    place, lane = lax.axis_index("dp"), lax.axis_index("tensor")
    x, core = place // CORES, place % CORES
    y, z = lane // SIDE, lane % SIDE
    pos = jnp.stack([x, core, y, z]).astype(jnp.int32)
    own_latents = latents.reshape(LAT, WIDTH)

    tanh_gate = jnp.tanh(gate_alpha)
    upstream = out_grad.astype(F32)
    own_branch_grad = (upstream * tanh_gate).astype(BF)
    cited = jnp.take(image_slot, citations, axis=0).reshape(-1)
    slots = cited.astype(jnp.int32)
    pos_slots = jnp.concatenate([pos, slots])

    gain_rows = jnp.broadcast_to(norm_gain[None, :], (EXTRA, WIDTH))
    packed = gather_ring(jnp.concatenate([text_hidden, own_latents, gain_rows], 0), send_z)
    text = jnp.stack([block[:ROWS] for block in packed])
    small = jnp.stack([block[ROWS:] for block in packed])
    grads = jnp.stack(gather_ring(own_branch_grad, send_y))
    text, small, pos, pos_slots = hold(text, small, pos, pos_slots)

    grads_above, grads_below = send_z(grads, -1), send_z(grads, 1)
    small = gather_direct(small, send_y)
    total = query_part(pos, [text], [(0, 0)], [(small[0], 0, LAT)], query_weight, (), False)
    text, total_a, total_b, *small = hold(text, *total, *small)
    total = (total_a, total_b)
    text_above, text_below = send_y(text, -1), send_y(text, 1)
    pair = own_pair(pos, small, [0] * SIDE, key_weight, value_weight)
    pair = lax.all_gather(pair, "dp", axis=0)
    slices_given, slices_kept = latent_slices(pos, small)
    slices_arrived = send_core(slices_given)
    grad_total = grad_part(pos, [grads], [(0, 0)], out_weight, (), False)
    text_above, text_below, grads_above, grads_below, pair, slices_arrived, *grad_total = hold(
        text_above, text_below, grads_above, grads_below, pair, slices_arrived, *grad_total
    )

    text_across, grads_across = send_y(text_below, 1), send_z(grads_below, 1)
    slices = jnp.stack([slices_kept, slices_arrived], 1)
    slices_3, slices_1 = send_x(slices[1], 1), send_x(slices[3], -1)
    slices = [slices[0], slices_1, send_x(slices[2], 2), slices_3]
    total = query_part(
        pos,
        [text_above, text_below],
        [(1, 0), (3, 0)],
        [(small[1], 0, LAT), (small[3], 0, LAT)],
        query_weight,
        total,
        False,
    )
    grad_total = grad_part(
        pos, [grads_above, grads_below], [(1, 0), (3, 0)], out_weight, grad_total, False
    )
    text_across, grads_across, total_a, total_b, *rest = hold(
        text_across, grads_across, *total, *grad_total, *slices
    )
    grad_total, slices = rest[:1], rest[1:]
    queries, inverse = query_part(
        pos,
        [text_across],
        [(2, 0)],
        [(small[2], 0, LAT)],
        query_weight,
        (total_a, total_b),
        True,
    )
    attended_grad = grad_part(pos, [grads_across], [(2, 0)], out_weight, grad_total, True)[0]
    all_text = [text, text_above, text_across, text_below]
    all_grads = [grads, grads_above, grads_across, grads_below]
    gains = jnp.concatenate([block[:, LAT] for block in small], 0)
    own_gain = []
    for half in range(2):
        t = place * 2 + half
        at = distance_to(pos, 2, t // SIDE) * SIDE + distance_to(pos, 3, t % SIDE)
        own_gain.append(lax.dynamic_index_in_dim(gains, at, 0, keepdims=False))
    own_gain = jnp.concatenate(own_gain).astype(F32)[:, None]

    attended, query_grad, scaled_grad, pair_kept, pair_given, row_dot = attention(
        pos_slots, queries, attended_grad, pair, inverse
    )

    def over_dp(term):
        return lax.psum_scatter(term, "dp", scatter_dimension=0, tiled=True)[0]

    out_weight_grad = over_dp(out_weight_terms(pos, attended, all_grads))
    query_weight_grad = over_dp(query_weight_terms(pos, scaled_grad, all_text))
    query_weight_grad = (query_weight_grad.astype(F32) * own_gain).astype(BF)

    near = add(pair_kept, send_core(pair_given)).astype(BF)
    (branch_2,) = branch_parts(pos, attended, out_weight, SIDE, [(2, 0)])
    (normed_2,) = normed_parts(pos, query_grad, row_dot, query_weight, SIDE, [(2, 0)])
    branch_2, normed_2, attended, query_grad, near = hold(
        branch_2, normed_2, attended, query_grad, near
    )
    branch_2, normed_2 = send_y(branch_2, 1), send_z(normed_2, 1)
    near_3, near_1, near_2 = send_x(near, 1), send_x(near, -1), send_x(near, 2)
    branch_1, branch_3 = branch_parts(pos, attended, out_weight, SIDE, [(1, 0), (3, 0)])
    normed_1, normed_3 = normed_parts(
        pos, query_grad, row_dot, query_weight, SIDE, [(1, 0), (3, 0)]
    )
    branch_1, normed_1 = add_arrived(pos, [branch_1, normed_1], [branch_2, normed_2])
    branch_1, branch_3, normed_1, normed_3, attended, query_grad, near_1, near_2, near_3 = hold(
        branch_1, branch_3, normed_1, normed_3, attended, query_grad, near_1, near_2, near_3
    )
    branch_1, normed_1 = send_y(branch_1, 1), send_z(normed_1, 1)
    branch_3, normed_3 = send_y(branch_3, -1), send_z(normed_3, -1)
    (branch_0,) = branch_parts(pos, attended, out_weight, SIDE, [(0, 0)])
    (normed_0,) = normed_parts(pos, query_grad, row_dot, query_weight, SIDE, [(0, 0)])
    near = add(
        near, jnp.roll(near_1, 1, axis=0), jnp.roll(near_2, 2, axis=0), jnp.roll(near_3, 3, axis=0)
    ).astype(BF)
    far = send_core(near)
    branch_0, branch_1, branch_3, normed_0, normed_1, normed_3, near, far = hold(
        branch_0, branch_1, branch_3, normed_0, normed_1, normed_3, near, far
    )

    def second(own, up, down, send):
        block = [add(own[k], up[k], down[k]) for k in range(SIDE)]
        sent = [value.astype(BF) for value in block]
        return add(block[0], send(sent[2], 2), send(sent[1], 1), send(sent[3], -1))

    branch = second(branch_0, branch_1, branch_3, send_z)
    normed_sum = second(normed_0, normed_1, normed_3, send_y)
    layer_out = (tanh_gate * branch).astype(BF)
    gate_part = jnp.sum(upstream * branch, axis=0) * (1.0 - tanh_gate * tanh_gate)

    key_weight_grad, value_weight_grad = latent_terms(pos, slices, near, far)

    normed_grad, row_sum = normed_sum[:ROWS], normed_sum[ROWS, :ROWS]
    inverse = inverse[:, :1]
    own_unit = text_hidden.astype(F32) * inverse
    unit_grad = normed_grad * norm_gain.astype(F32)
    text_grad = ((unit_grad - own_unit * (row_sum / D)[:, None]) * inverse).astype(BF)
    gain_part = jnp.sum(normed_grad * own_unit, axis=0)
    sums = jnp.stack([gain_part, gate_part])
    sums = sums + send_core(sums)
    sums = sums + send_x(sums, 1) + send_x(sums, -1) + send_x(sums, 2)
    return (
        layer_out,
        text_grad,
        query_weight_grad,
        key_weight_grad,
        value_weight_grad,
        out_weight_grad,
        sums[0],
        sums[1],
    )


def solution(mesh):
    placed = (
        P("dp", "tensor"),
        P("tensor"),
        P("tensor"),
        P("dp", None, "tensor"),
        P(None, "tensor"),
        P(None, "tensor"),
        P(None, "tensor"),
        P("tensor", None),
        P("dp", None),
        P(),
        P("dp", "tensor"),
    )
    return jax.shard_map(
        shards,
        mesh=mesh,
        in_specs=placed,
        out_specs=(
            P("dp", "tensor"),
            P("dp", "tensor"),
            P("dp", "tensor"),
            P("dp", "tensor"),
            P("dp", "tensor"),
            P("tensor", "dp"),
            P("tensor"),
            P("tensor"),
        ),
        check_vma=False,
    )
```

time: 310 us -> 220 us (0.71)
  waiting for transfers between devices: 110 us -> 50.1 us
  starting transfers between devices: 89.9 us -> 51.3 us
  between operations: 1.39 us -> 18.1 us
  other arithmetic: 26.8 us -> 12.6 us
  blocking collectives: 0 us -> 13.5 us
  local copies, waits for them, and re-layouts: 33.2 us -> 28.8 us
    ppermute x50 -> x36, waiting for transfers between devices: 110 us -> 49 us  [ring_send(): return lax.ppermute(value, ('dp', 'tensor'), moves)]
    ppermute x50 -> x36, starting transfers between devices: 88.5 us -> 48.2 us  [ring_send(): return lax.ppermute(value, ('dp', 'tensor'), moves)]
    all_gather x0 -> x1, blocking collectives: none -> 13.5 us  [shards(): pair = lax.all_gather(pair, 'dp', axis=0)]
    convert_element_type x9 -> x3, other arithmetic: 7.24 us -> 2.18 us  [the longest x1 2.04 us: shards(): query_weight_grad = (query_weight_grad.astype(F32) * own_gain).astype(BF)]
    concatenate x5 -> x2, other arithmetic: 5.36 us -> 1.03 us  [the longest x1 1.01 us: shards(): jnp.concatenate([text_hidden, own_latents, gain_rows], 0)]
    slice x15 -> x10, local copies, waits for them, and re-layouts: 9.35 us -> 5.72 us  [the longest x4 2.31 us: shards(): gains = jnp.concatenate([block[:, LAT] for block in small], 0)]
    unnamed x55 -> x96, local copies, waits for them, and re-layouts: 18.4 us -> 19.9 us
  transfers between devices with their start and end apart: 56 -> 42, of which waited for: 20 -> 21; matrix products, arithmetic and copies ran while one was open for 15% -> 9% of each run, Pallas kernels for 13% -> 16%
where the time goes in v1:
time: 220 us; the launch traced here: 219 us
  starting transfers between devices  51.3 us (23%)
  waiting for transfers between devices  50.1 us (23%)
  Pallas kernels  44.8 us (20%)
  local copies, waits for them, and re-layouts  28.8 us (13%)
  between operations  18.1 us (8%)
  blocking collectives  13.5 us (6%)
  other arithmetic  12.6 us (6%)
    ppermute x36, waiting for transfers between devices, ring_send(): return lax.ppermute(value, ('dp', 'tensor'), moves)  49 us
    ppermute x36, starting transfers between devices, ring_send(): return lax.ppermute(value, ('dp', 'tensor'), moves)  48.2 us
    pallas_call x19, Pallas kernels, call(): pl.pallas_call(body, grid_spec=pltpu.PrefetchScalarGridSpec(num_scalar_pr...  44.8 us
    unnamed x96, local copies, waits for them, and re-layouts  19.9 us
    all_gather x1, blocking collectives, shards(): pair = lax.all_gather(pair, 'dp', axis=0)  13.5 us
  transfers between devices with their start and end apart: 42, of which 21 were waited for; matrix products, arithmetic and copies ran while one was open for 9% of the time, Pallas kernels for 16%

profile of v1, /device:TPU:0, one launch (start us, length us, event | category | flops | bytes accessed | tf_op | source)
XLA Modules:
  0.0 219.0 jit_solution(8877202247472202212)
XLA Ops:
  9.0 3.2 %collective-permute-start.8 = (bf16[256,512]{1,0:T(8,128)(2,1)S(1)}, bf16[256,512]{1,0:T(8,128)(2,1)S(1)}, u32[]{:S(2)}, u32[]{:S(2)}) collective-permute-start(bf16[256,512]{1,0:T(8,128)(2,1)S(1)} %fusion.3), channel_id=1, source_target_pairs={{0,12},{1,13},{2,14},{3,15},{4,0},{5,1},{6,2},{7,3},{8,4},{9,5},{1... | collective-permute-start | bytes 786440 | tf_op jit(solution)/shard_map/ppermute | solution.py:42
  19.8 5.4 %collective-permute-done.1 = bf16[336,512]{1,0:T(8,128)(2,1)S(1)} collective-permute-done((bf16[336,512]{1,0:T(8,128)(2,1)S(1)}, bf16[336,512]{1,0:T(8,128)(2,1)S(1)}, u32[]{:S(2)}, u32[]{:S(2)}) %collective-permute-start.1) | collective-permute-done | bytes 344096 | tf_op jit(solution)/shard_map/ppermute | solution.py:42
  26.1 7.6 %collective-permute-done.2 = bf16[336,512]{1,0:T(8,128)(2,1)S(1)} collective-permute-done((bf16[336,512]{1,0:T(8,128)(2,1)S(1)}, bf16[336,512]{1,0:T(8,128)(2,1)S(1)}, u32[]{:S(2)}, u32[]{:S(2)}) %collective-permute-start.2) | collective-permute-done | bytes 344096 | tf_op jit(solution)/shard_map/ppermute | solution.py:42
  34.9 5.4 %collective-permute-start.4 = (bf16[4,80,512]{2,1,0:T(8,128)(2,1)S(1)}, bf16[4,80,512]{2,1,0:T(8,128)(2,1)S(1)}, u32[]{:S(2)}, u32[]{:S(2)}) collective-permute-start(bf16[4,80,512]{2,1,0:T(8,128)(2,1)S(1)} %pad_maximum_fusion.3.refs_1_.refs_0_), channel_id=1, source_target_pairs={{0,8},{1,9},{2,10},{3,11},{4,12},{5,13},{6,14},{7,15},{8,0},{9,1},... | collective-permute-start | bytes 983048 | tf_op jit(solution)/shard_map/ppermute | solution.py:42
  40.6 3.2 %collective-permute-start.11 = (bf16[4,256,512]{2,1,0:T(8,128)(2,1)S(1)}, bf16[4,256,512]{2,1,0:T(8,128)(2,1)S(1)}, u32[]{:S(2)}, u32[]{:S(2)}) collective-permute-start(bf16[4,256,512]{2,1,0:T(8,128)(2,1)S(1)} %pad_maximum_fusion.1.refs_0_), channel_id=1, source_target_pairs={{0,3},{1,0},{2,1},{3,2},{4,7},{5,4},{6,5},{7,6},{8,11},{9,8},{10,9... | collective-permute-start | bytes 3145736 | tf_op jit(solution)/shard_map/ppermute | solution.py:42
  46.4 3.6 %collective-permute-done.4.refs_2_.refs_1_ = bf16[4,80,512]{2,1,0:T(8,128)(2,1)S(1)} collective-permute-done((bf16[4,80,512]{2,1,0:T(8,128)(2,1)S(1)}, bf16[4,80,512]{2,1,0:T(8,128)(2,1)S(1)}, u32[]{:S(2)}, u32[]{:S(2)}) %collective-permute-start.4) | collective-permute-done | bytes 327712 | tf_op jit(solution)/shard_map/ppermute | solution.py:42
  50.0 3.2 %collective-permute-start.6 = (bf16[4,256,512]{2,1,0:T(8,128)(2,1)S(1)}, bf16[4,256,512]{2,1,0:T(8,128)(2,1)S(1)}, u32[]{:S(2)}, u32[]{:S(2)}) collective-permute-start(bf16[4,256,512]{2,1,0:T(8,128)(2,1)S(1)} %pad_maximum_fusion.refs_0_), channel_id=1, source_target_pairs={{0,12},{1,13},{2,14},{3,15},{4,0},{5,1},{6,2},{7,3},{8,4},{9,5},{1... | collective-permute-start | bytes 3145736 | tf_op jit(solution)/shard_map/ppermute | solution.py:42
  58.8 2.8 %shard_map.171 = bf16[64,512]{1,0:T(8,128)(2,1)S(1)} custom-call(s32[4]{0:T(128)S(1)} %pad_add_fusion.pos, bf16[4,80,512]{2,1,0:T(8,128)(2,1)S(1)} %pad_maximum_fusion.3.refs_1_.refs_0_, bf16[4,80,512]{2,1,0:T(8,128)(2,1)S(1)} %collective-permute-done.3.refs_1_.refs_2_, bf16[4,80,512]{2,1,0:T(8,128)(2,1)S(1)} %collective-permute-done.4.refs_2_.refs_1_, ...), custom_call_target="tpu_custom_call" | custom-call | flops 8388608 | bytes 163840 | tf_op jit(solution)/shard_map/pallas_call | solution.py:90
  61.6 13.5 %all-gather = bf16[512,512]{1,0:T(8,128)(2,1)S(1)} all-gather(bf16[64,512]{1,0:T(8,128)(2,1)S(1)} %shard_map.171), channel_id=2, replica_groups=mesh['dp'=8,'tensor'=16] {'dp'}, dimensions={0}, use_global_device_ids=true | all-gather | bytes 589824 | tf_op jit(solution)/shard_map/all_gather | solution.py:497
  86.1 4.5 %collective-permute-done.17.refs_2_ = bf16[2,64,1024]{2,1,0:T(8,128)(2,1)S(1)} collective-permute-done((bf16[2,64,1024]{2,1,0:T(8,128)(2,1)S(1)}, bf16[2,64,1024]{2,1,0:T(8,128)(2,1)S(1)}, u32[]{:S(2)}, u32[]{:S(2)}) %collective-permute-start.17) | collective-permute-done | bytes 262176 | tf_op jit(solution)/shard_map/ppermute | solution.py:42
  95.0 2.9 %shard_map.178 = (bf16[256,256]{1,0:T(8,128)(2,1)S(1)}, bf16[256,256]{1,0:T(8,128)(2,1)S(1)}, bf16[256,256]{1,0:T(8,128)(2,1)S(1)}, bf16[4,64,512]{2,1,0:T(8,128...) custom-call(s32[12]{0:T(128)S(1)} %concatenate.38.pos, ...), custom_call_target="tpu_custom_call" | custom-call | flops 5242880 | bytes 49152 | tf_op jit(solution)/shard_map/pallas_call | solution.py:90
  100.7 3.0 %shard_map.186 = bf16[4,2,1024,256]{3,2,1,0:T(8,128)(2,1)S(1)} custom-call(s32[4]{0:T(128)S(1)} %pad_add_fusion.pos, bf16[256,256]{1,0:T(8,128)(2,1)S(1)} %get-tuple-element.141.query_grad, bf16[4,256,512]{2,1,0:T(8,128)(2,1)S(1)} %pad_maximum_fusion.refs_0_, bf16[4,256,512]{2,1,0:T(8,128)(2,1)S(1)} %collective-permute-done.6.refs_0_.refs_1_, ...), custom_call_target="tpu_custom_call" | custom-call | flops 16777216 | bytes 131072 | tf_op jit(solution)/shard_map/pallas_call | solution.py:90
  113.4 2.7 %collective-permute-start.19 = (bf16[4,64,512]{2,1,0:T(8,128)(2,1)S(1)}, bf16[4,64,512]{2,1,0:T(8,128)(2,1)S(1)}, u32[]{:S(2)}, u32[]{:S(2)}) collective-permute-start(bf16[4,64,512]{2,1,0:T(8,128)(2,1)S(1)} %copy-done.38), channel_id=1, source_target_pairs={{0,16},{16,0},{32,48},{48,32},{64,80},{80,64},{96,112},{112,96},{1... | collective-permute-start | bytes 786440 | tf_op jit(solution)/shard_map/ppermute | solution.py:51
  118.3 2.8 %shard_map.179 = bf16[4,256,512]{2,1,0:T(8,128)(2,1)} custom-call(s32[4]{0:T(128)S(1)} %pad_add_fusion.pos, bf16[256,256]{1,0:T(8,128)(2,1)S(1)} %copy-done.21, bf16[256,8192]{1,0:T(8,128)(2,1)S(1)} %copy-done.3), custom_call_target="tpu_custom_call" | custom-call | flops 4194304 | bytes 32768 | tf_op jit(solution)/shard_map/pallas_call | solution.py:90
  124.6 3.4 %collective-permute-start.23 = (bf16[4,64,512]{2,1,0:T(8,128)(2,1)S(1)}, bf16[4,64,512]{2,1,0:T(8,128)(2,1)}, u32[]{:S(2)}, u32[]{:S(2)}) collective-permute-start(bf16[4,64,512]{2,1,0:T(8,128)(2,1)S(1)} %add_convert_fusion.7), channel_id=1, source_target_pairs={{0,64},{1,65},{2,66},{3,67},{4,68},{5,69},{6,70},{7,71},{8,72},{9,... | collective-permute-start | bytes 786440 | tf_op jit(solution)/shard_map/ppermute | solution.py:42
  130.5 3.2 %shard_map.181 = (bf16[4,256,512]{2,1,0:T(8,128)(2,1)}, bf16[4,256,512]{2,1,0:T(8,128)(2,1)}) custom-call(s32[4]{0:T(128)S(1)} %pad_add_fusion.pos, bf16[256,256]{1,0:T(8,128)(2,1)S(1)} %copy-done.21, bf16[256,8192]{1,0:T(8,128)(2,1)S(1)} %copy-done.4, bf16[256,8192]{1,0:T(8,128)(2,1)S(1)} %copy-done.4), custom_call_target="tpu_custom_call" | custom-call | flops 8388608 | bytes 65536 | tf_op jit(solution)/shard_map/pallas_call | solution.py:90
  133.8 3.1 %shard_map.182 = (bf16[4,272,512]{2,1,0:T(8,128)(2,1)}, bf16[4,272,512]{2,1,0:T(8,128)(2,1)}) custom-call(s32[4]{0:T(128)S(1)} %pad_add_fusion.pos, bf16[256,256]{1,0:T(8,128)(2,1)S(1)} %copy-done.23, bf16[8192,256]{1,0:T(8,128)(2,1)S(1)} %copy-done.8, bf16[8192,256]{1,0:T(8,128)(2,1)S(1)} %copy-done.8, bf16[16,512]{1,0:T(8,128)(2,1)S(1)} %copy-done.36), custom_call_target="tpu_custom_call" | custom-call | flops 8388608 | bytes 65536 | tf_op jit(solution)/shard_map/pallas_call | solution.py:90
  136.9 3.2 %collective-permute-done.20.refs_2_ = bf16[4,256,512]{2,1,0:T(8,128)(2,1)S(1)} collective-permute-done((bf16[4,256,512]{2,1,0:T(8,128)(2,1)}, bf16[4,256,512]{2,1,0:T(8,128)(2,1)S(1)}, u32[]{:S(2)}, u32[]{:S(2)}) %collective-permute-start.20) | collective-permute-done | bytes 1048608 | tf_op jit(solution)/shard_map/ppermute | solution.py:42
  140.0 4.6 %shard_map.183 = (bf16[4,256,512]{2,1,0:T(8,128)(2,1)}, bf16[4,272,512]{2,1,0:T(8,128)(2,1)}) custom-call(s32[4]{0:T(128)S(1)} %pad_add_fusion.pos, bf16[4,256,512]{2,1,0:T(8,128)(2,1)} %get-tuple-element.116.refs_0_, bf16[4,272,512]{2,1,0:T(8,128)(2,1)} %get-tuple-element.118.refs_1_, ...), custom_call_target="tpu_custom_call", output_to_operand_aliasing={{0}: (1, {}), {1}: (2, {})} | custom-call | flops 16384 | bytes 98304 | tf_op jit(solution)/shard_map/pallas_call | solution.py:90
  147.1 2.7 %collective-permute-start.26 = (bf16[4,256,512]{2,1,0:T(8,128)(2,1)}, bf16[4,256,512]{2,1,0:T(8,128)(2,1)}, u32[]{:S(2)}, u32[]{:S(2)}) collective-permute-start(bf16[4,256,512]{2,1,0:T(8,128)(2,1)} %get-tuple-element.128), channel_id=1, source_target_pairs={{0,12},{1,13},{2,14},{3,15},{4,0},{5,1},{6,2},{7,3},{8,4},{9,5},{1... | collective-permute-start | bytes 3145736 | tf_op jit(solution)/shard_map/ppermute | solution.py:42
  168.8 5.1 %collective-permute-done.25 = bf16[4,256,512]{2,1,0:T(8,128)(2,1)S(1)} collective-permute-done((bf16[4,256,512]{2,1,0:T(8,128)(2,1)}, bf16[4,256,512]{2,1,0:T(8,128)(2,1)S(1)}, u32[]{:S(2)}, u32[]{:S(2)}) %collective-permute-start.25) | collective-permute-done | bytes 1048608 | tf_op jit(solution)/shard_map/ppermute | solution.py:42
  185.0 3.1 %collective-permute-done.30 = bf16[256,512]{1,0:T(8,128)(2,1)S(1)} collective-permute-done((bf16[256,512]{1,0:T(8,128)(2,1)S(1)}, bf16[256,512]{1,0:T(8,128)(2,1)S(1)}, u32[]{:S(2)}, u32[]{:S(2)}) %collective-permute-start.30) | collective-permute-done | bytes 262176 | tf_op jit(solution)/shard_map/ppermute | solution.py:42
  192.8 5.0 %collective-permute-done.35 = bf16[272,512]{1,0:T(8,128)(2,1)S(1)} collective-permute-done((bf16[272,512]{1,0:T(8,128)(2,1)S(1)}, bf16[272,512]{1,0:T(8,128)(2,1)S(1)}, u32[]{:S(2)}, u32[]{:S(2)}) %collective-permute-start.35) | collective-permute-done | bytes 278560 | tf_op jit(solution)/shard_map/ppermute | solution.py:42
  201.3 2.7 %collective-permute-start.38 = (f32[2,512]{1,0:T(2,128)S(1)}, f32[2,512]{1,0:T(2,128)S(1)}, u32[]{:S(2)}, u32[]{:S(2)}) collective-permute-start(f32[2,512]{1,0:T(2,128)S(1)} %fusion.20), channel_id=1, source_target_pairs={{0,96},{1,97},{2,98},{3,99},{4,100},{5,101},{6,102},{7,103},{8,104... | collective-permute-start | bytes 12296 | tf_op jit(solution)/shard_map/ppermute | solution.py:42
  (232 shorter events, 101.1 us)
Async XLA Ops:
  7.2 203.0 %reduce-scatter.3.cloned.1.call-start = ((), (), s32[]{:S(2)}) async-start(), calls=%async_computation.2 | async-start | bytes 4718592 | tf_op jit(solution)/shard_map/reduce_scatter | solution.py:550
  9.0 31.4 %collective-permute-start.8 = (bf16[256,512]{1,0:T(8,128)(2,1)S(1)}, bf16[256,512]{1,0:T(8,128)(2,1)S(1)}, u32[]{:S(2)}, u32[]{:S(2)}) collective-permute-start(bf16[256,512]{1,0:T(8,128)(2,1)S(1)} %fusion.3), channel_id=1, source_target_pairs={{0,12},{1,13},{2,14},{3,15},{4,0},{5,1},{6,2},{7,3},{8,4},{9,5},{1... | collective-permute-start | bytes 786440 | tf_op jit(solution)/shard_map/ppermute | solution.py:42
  13.8 11.3 %collective-permute-start.1 = (bf16[336,512]{1,0:T(8,128)(2,1)S(1)}, bf16[336,512]{1,0:T(8,128)(2,1)S(1)}, u32[]{:S(2)}, u32[]{:S(2)}) collective-permute-start(bf16[336,512]{1,0:T(8,128)(2,1)S(1)} %pad_maximum_fusion.2), channel_id=1, source_target_pairs={{0,1},{1,2},{2,3},{3,0},{4,5},{5,6},{6,7},{7,4},{8,9},{9,10},{10,1... | collective-permute-start | bytes 1032200 | tf_op jit(solution)/shard_map/ppermute | solution.py:42
  19.7 20.7 %collective-permute-start.10 = (bf16[256,512]{1,0:T(8,128)(2,1)S(1)}, bf16[256,512]{1,0:T(8,128)(2,1)S(1)}, u32[]{:S(2)}, u32[]{:S(2)}) collective-permute-start(bf16[256,512]{1,0:T(8,128)(2,1)S(1)} %collective-permute-done.9), channel_id=1, source_target_pairs={{0,4},{1,5},{2,6},{3,7},{4,8},{5,9},{6,10},{7,11},{8,12},{9,13},{1... | collective-permute-start | bytes 786440 | tf_op jit(solution)/shard_map/ppermute | solution.py:42
  33.9 12.5 %collective-permute-start.5 = (bf16[4,80,512]{2,1,0:T(8,128)(2,1)S(1)}, bf16[4,80,512]{2,1,0:T(8,128)(2,1)S(1)}, u32[]{:S(2)}, u32[]{:S(2)}) collective-permute-start(bf16[4,80,512]{2,1,0:T(8,128)(2,1)S(1)} %pad_maximum_fusion.3.refs_1_.refs_0_), channel_id=1, source_target_pairs={{0,4},{1,5},{2,6},{3,7},{4,8},{5,9},{6,10},{7,11},{8,12},{9,13},{1... | collective-permute-start | bytes 983048 | tf_op jit(solution)/shard_map/ppermute | solution.py:42
  34.9 15.0 %collective-permute-start.4 = (bf16[4,80,512]{2,1,0:T(8,128)(2,1)S(1)}, bf16[4,80,512]{2,1,0:T(8,128)(2,1)S(1)}, u32[]{:S(2)}, u32[]{:S(2)}) collective-permute-start(bf16[4,80,512]{2,1,0:T(8,128)(2,1)S(1)} %pad_maximum_fusion.3.refs_1_.refs_0_), channel_id=1, source_target_pairs={{0,8},{1,9},{2,10},{3,11},{4,12},{5,13},{6,14},{7,15},{8,0},{9,1},... | collective-permute-start | bytes 983048 | tf_op jit(solution)/shard_map/ppermute | solution.py:42
  40.5 34.6 %collective-permute-start.12 = (bf16[4,256,512]{2,1,0:T(8,128)(2,1)S(1)}, bf16[4,256,512]{2,1,0:T(8,128)(2,1)S(1)}, u32[]{:S(2)}, u32[]{:S(2)}) collective-permute-start(bf16[4,256,512]{2,1,0:T(8,128)(2,1)S(1)} %pad_maximum_fusion.1.refs_0_), channel_id=1, source_target_pairs={{0,1},{1,2},{2,3},{3,0},{4,5},{5,6},{6,7},{7,4},{8,9},{9,10},{10,1... | collective-permute-start | bytes 3145736 | tf_op jit(solution)/shard_map/ppermute | solution.py:42
  40.6 34.5 %collective-permute-start.11 = (bf16[4,256,512]{2,1,0:T(8,128)(2,1)S(1)}, bf16[4,256,512]{2,1,0:T(8,128)(2,1)S(1)}, u32[]{:S(2)}, u32[]{:S(2)}) collective-permute-start(bf16[4,256,512]{2,1,0:T(8,128)(2,1)S(1)} %pad_maximum_fusion.1.refs_0_), channel_id=1, source_target_pairs={{0,3},{1,0},{2,1},{3,2},{4,7},{5,4},{6,5},{7,6},{8,11},{9,8},{10,9... | collective-permute-start | bytes 3145736 | tf_op jit(solution)/shard_map/ppermute | solution.py:42
  49.9 25.2 %collective-permute-start.7 = (bf16[4,256,512]{2,1,0:T(8,128)(2,1)S(1)}, bf16[4,256,512]{2,1,0:T(8,128)(2,1)S(1)}, u32[]{:S(2)}, u32[]{:S(2)}) collective-permute-start(bf16[4,256,512]{2,1,0:T(8,128)(2,1)S(1)} %pad_maximum_fusion.refs_0_), channel_id=1, source_target_pairs={{0,4},{1,5},{2,6},{3,7},{4,8},{5,9},{6,10},{7,11},{8,12},{9,13},{1... | collective-permute-start | bytes 3145736 | tf_op jit(solution)/shard_map/ppermute | solution.py:42
  50.0 25.1 %collective-permute-start.6 = (bf16[4,256,512]{2,1,0:T(8,128)(2,1)S(1)}, bf16[4,256,512]{2,1,0:T(8,128)(2,1)S(1)}, u32[]{:S(2)}, u32[]{:S(2)}) collective-permute-start(bf16[4,256,512]{2,1,0:T(8,128)(2,1)S(1)} %pad_maximum_fusion.refs_0_), channel_id=1, source_target_pairs={{0,12},{1,13},{2,14},{3,15},{4,0},{5,1},{6,2},{7,3},{8,4},{9,5},{1... | collective-permute-start | bytes 3145736 | tf_op jit(solution)/shard_map/ppermute | solution.py:42
  54.3 20.8 %collective-permute-start.13 = (bf16[4,64,1024]{2,1,0:T(8,128)(2,1)S(1)}, bf16[4,64,1024]{2,1,0:T(8,128)(2,1)S(1)}, u32[]{:S(2)}, u32[]{:S(2)}) collective-permute-start(bf16[4,64,1024]{2,1,0:T(8,128)(2,1)S(1)} %get-tuple-element.90), channel_id=1, source_target_pairs={{0,16},{16,0},{32,48},{48,32},{64,80},{80,64},{96,112},{112,96},{1... | collective-permute-start | bytes 1572872 | tf_op jit(solution)/shard_map/ppermute | solution.py:51
  75.1 16.1 %collective-permute-start.14 = (bf16[4,256,512]{2,1,0:T(8,128)(2,1)S(1)}, bf16[4,256,512]{2,1,0:T(8,128)(2,1)S(1)}, u32[]{:S(2)}, u32[]{:S(2)}) collective-permute-start(bf16[4,256,512]{2,1,0:T(8,128)(2,1)S(1)} %collective-permute-done.7.refs_1_.refs_3_), channel_id=1, source_target_pairs={{0,4},{1,5},{2,6},{3,7},{4,8},{5,9},{6,10},{7,11},{8,12},{9,13},{1... | collective-permute-start | bytes 3145736 | tf_op jit(solution)/shard_map/ppermute | solution.py:42
  75.2 16.2 %collective-permute-start.15 = (bf16[4,256,512]{2,1,0:T(8,128)(2,1)S(1)}, bf16[4,256,512]{2,1,0:T(8,128)(2,1)S(1)}, u32[]{:S(2)}, u32[]{:S(2)}) collective-permute-start(bf16[4,256,512]{2,1,0:T(8,128)(2,1)S(1)} %collective-permute-done.12.refs_1_.refs_3_), channel_id=1, source_target_pairs={{0,1},{1,2},{2,3},{3,0},{4,5},{5,6},{6,7},{7,4},{8,9},{9,10},{10,1... | collective-permute-start | bytes 3145736 | tf_op jit(solution)/shard_map/ppermute | solution.py:42
  105.8 106.4 %reduce-scatter.5.cloned.1.call-start = ((), (), s32[]{:S(2)}) async-start(), calls=%async_computation.3 | async-start | bytes 4718592 | tf_op jit(solution)/shard_map/reduce_scatter | solution.py:550
  122.9 17.2 %collective-permute-start.21 = (bf16[4,272,512]{2,1,0:T(8,128)(2,1)S(1)}, bf16[4,272,512]{2,1,0:T(8,128)(2,1)}, u32[]{:S(2)}, u32[]{:S(2)}) collective-permute-start(bf16[4,272,512]{2,1,0:T(8,128)(2,1)S(1)} %shard_map.180), channel_id=1, source_target_pairs={{0,1},{1,2},{2,3},{3,0},{4,5},{5,6},{6,7},{7,4},{8,9},{9,10},{10,1... | collective-permute-start | bytes 3342344 | tf_op jit(solution)/shard_map/ppermute | solution.py:42
  123.8 16.2 %collective-permute-start.20 = (bf16[4,256,512]{2,1,0:T(8,128)(2,1)}, bf16[4,256,512]{2,1,0:T(8,128)(2,1)S(1)}, u32[]{:S(2)}, u32[]{:S(2)}) collective-permute-start(bf16[4,256,512]{2,1,0:T(8,128)(2,1)} %shard_map.179), channel_id=1, source_target_pairs={{0,4},{1,5},{2,6},{3,7},{4,8},{5,9},{6,10},{7,11},{8,12},{9,13},{1... | collective-permute-start | bytes 3145736 | tf_op jit(solution)/shard_map/ppermute | solution.py:42
  124.6 20.1 %collective-permute-start.24 = (bf16[4,64,512]{2,1,0:T(8,128)(2,1)S(1)}, bf16[4,64,512]{2,1,0:T(8,128)(2,1)S(1)}, u32[]{:S(2)}, u32[]{:S(2)}) collective-permute-start(bf16[4,64,512]{2,1,0:T(8,128)(2,1)S(1)} %add_convert_fusion.7), channel_id=1, source_target_pairs={{0,32},{1,33},{2,34},{3,35},{4,36},{5,37},{6,38},{7,39},{8,40},{9,... | collective-permute-start | bytes 786440 | tf_op jit(solution)/shard_map/ppermute | solution.py:42
  124.6 20.5 %collective-permute-start.23 = (bf16[4,64,512]{2,1,0:T(8,128)(2,1)S(1)}, bf16[4,64,512]{2,1,0:T(8,128)(2,1)}, u32[]{:S(2)}, u32[]{:S(2)}) collective-permute-start(bf16[4,64,512]{2,1,0:T(8,128)(2,1)S(1)} %add_convert_fusion.7), channel_id=1, source_target_pairs={{0,64},{1,65},{2,66},{3,67},{4,68},{5,69},{6,70},{7,71},{8,72},{9,... | collective-permute-start | bytes 786440 | tf_op jit(solution)/shard_map/ppermute | solution.py:42
  128.0 18.6 %collective-permute-start.22 = (bf16[4,64,512]{2,1,0:T(8,128)(2,1)S(1)}, bf16[4,64,512]{2,1,0:T(8,128)(2,1)}, u32[]{:S(2)}, u32[]{:S(2)}) collective-permute-start(bf16[4,64,512]{2,1,0:T(8,128)(2,1)S(1)} %add_convert_fusion.7), channel_id=1, source_target_pairs={{0,96},{1,97},{2,98},{3,99},{4,100},{5,101},{6,102},{7,103},{8,104... | collective-permute-start | bytes 786440 | tf_op jit(solution)/shard_map/ppermute | solution.py:42
  146.6 27.4 %collective-permute-start.25 = (bf16[4,256,512]{2,1,0:T(8,128)(2,1)}, bf16[4,256,512]{2,1,0:T(8,128)(2,1)S(1)}, u32[]{:S(2)}, u32[]{:S(2)}) collective-permute-start(bf16[4,256,512]{2,1,0:T(8,128)(2,1)} %get-tuple-element.127), channel_id=1, source_target_pairs={{0,4},{1,5},{2,6},{3,7},{4,8},{5,9},{6,10},{7,11},{8,12},{9,13},{1... | collective-permute-start | bytes 3145736 | tf_op jit(solution)/shard_map/ppermute | solution.py:42
  147.1 26.9 %collective-permute-start.26 = (bf16[4,256,512]{2,1,0:T(8,128)(2,1)}, bf16[4,256,512]{2,1,0:T(8,128)(2,1)}, u32[]{:S(2)}, u32[]{:S(2)}) collective-permute-start(bf16[4,256,512]{2,1,0:T(8,128)(2,1)} %get-tuple-element.128), channel_id=1, source_target_pairs={{0,12},{1,13},{2,14},{3,15},{4,0},{5,1},{6,2},{7,3},{8,4},{9,5},{1... | collective-permute-start | bytes 3145736 | tf_op jit(solution)/shard_map/ppermute | solution.py:42
  149.8 26.1 %collective-permute-start.27 = (bf16[4,272,512]{2,1,0:T(8,128)(2,1)}, bf16[4,272,512]{2,1,0:T(8,128)(2,1)S(1)}, u32[]{:S(2)}, u32[]{:S(2)}) collective-permute-start(bf16[4,272,512]{2,1,0:T(8,128)(2,1)} %get-tuple-element.130), channel_id=1, source_target_pairs={{0,1},{1,2},{2,3},{3,0},{4,5},{5,6},{6,7},{7,4},{8,9},{9,10},{10,1... | collective-permute-start | bytes 3342344 | tf_op jit(solution)/shard_map/ppermute | solution.py:42
  151.5 24.4 %collective-permute-start.28 = (bf16[4,272,512]{2,1,0:T(8,128)(2,1)}, bf16[4,272,512]{2,1,0:T(8,128)(2,1)}, u32[]{:S(2)}, u32[]{:S(2)}) collective-permute-start(bf16[4,272,512]{2,1,0:T(8,128)(2,1)} %get-tuple-element.131), channel_id=1, source_target_pairs={{0,3},{1,0},{2,1},{3,2},{4,7},{5,4},{6,5},{7,6},{8,11},{9,8},{10,9... | collective-permute-start | bytes 3342344 | tf_op jit(solution)/shard_map/ppermute | solution.py:42
  183.3 14.6 %collective-permute-start.35 = (bf16[272,512]{1,0:T(8,128)(2,1)S(1)}, bf16[272,512]{1,0:T(8,128)(2,1)S(1)}, u32[]{:S(2)}, u32[]{:S(2)}) collective-permute-start(bf16[272,512]{1,0:T(8,128)(2,1)S(1)} %get-tuple-element.155), channel_id=1, source_target_pairs={{0,12},{1,13},{2,14},{3,15},{4,0},{5,1},{6,2},{7,3},{8,4},{9,5},{1... | collective-permute-start | bytes 835592 | tf_op jit(solution)/shard_map/ppermute | solution.py:42
  (65 other events, 500.8 us)
Sparse Core Ops, SparseCore 0:
  105.9 47.5 reduce-scatter.2
  156.5 37.4 reduce-scatter.4

commit v2 on v1

--- a/solution.py
+++ b/solution.py
@@ -98,7 +98,7 @@
         ),
         out_shape=list(shapes),
         compiler_params=pltpu.CompilerParams(
-            dimension_semantics=("arbitrary",) * len(grid), vmem_limit_bytes=24 * 2**20
+            dimension_semantics=("arbitrary",) * len(grid), vmem_limit_bytes=12 * 2**20
         ),
         input_output_aliases=aliases or {},
         cost_estimate=pl.CostEstimate(flops=flops // COST, bytes_accessed=moved // COST, transcendentals=0),
@@ -390,25 +390,6 @@
     return out.reshape(8, 2 * WIDTH, COLS)
 
 
-def add_body(count, pos, *refs):
-    sums, terms, outs = refs[:count], refs[count : 2 * count], refs[2 * count :]
-    for total, term, out in zip(sums, terms, outs):
-        out[...] = (total[...].astype(F32) + term[...].astype(F32)).astype(BF)
-
-
-def add_arrived(pos, sums, terms):
-    ins, outs = [], []
-    for total in sums:
-        spec = pl.BlockSpec((1,) + total.shape[1:], lambda i, pos: (i, 0, 0))
-        ins.append((total, spec))
-        outs.append((jax.ShapeDtypeStruct(total.shape, BF), spec))
-    for term in terms:
-        ins.append((term, pl.BlockSpec((1,) + term.shape[1:], lambda i, pos: (i, 0, 0))))
-    body = functools.partial(add_body, len(sums))
-    aliases = {1 + i: i for i in range(len(sums))}
-    return call(body, pos, (SIDE,), ins, outs, [], 2**20, 6 * 2**20, aliases)
-
-
 def slice_body(pos, *refs):
     given, kept = refs[-2:]
     for ky in range(SIDE):
@@ -560,15 +541,16 @@
         branch_2, normed_2, attended, query_grad, near
     )
     branch_2, normed_2 = send_y(branch_2, 1), send_z(normed_2, 1)
-    near_3, near_1, near_2 = send_x(near, 1), send_x(near, -1), send_x(near, 2)
+    near_3, near_1 = send_x(near, 1), send_x(near, -1)
     branch_1, branch_3 = branch_parts(pos, attended, out_weight, SIDE, [(1, 0), (3, 0)])
     normed_1, normed_3 = normed_parts(
         pos, query_grad, row_dot, query_weight, SIDE, [(1, 0), (3, 0)]
     )
-    branch_1, normed_1 = add_arrived(pos, [branch_1, normed_1], [branch_2, normed_2])
-    branch_1, branch_3, normed_1, normed_3, attended, query_grad, near_1, near_2, near_3 = hold(
-        branch_1, branch_3, normed_1, normed_3, attended, query_grad, near_1, near_2, near_3
-    )
+    branch_1, normed_1 = add(branch_1, branch_2).astype(BF), add(normed_1, normed_2).astype(BF)
+    branch_1, branch_3, normed_1, normed_3, attended, query_grad, near, near_1, near_3 = hold(
+        branch_1, branch_3, normed_1, normed_3, attended, query_grad, near, near_1, near_3
+    )
+    near_2 = send_x(near, 2)
     branch_1, normed_1 = send_y(branch_1, 1), send_z(normed_1, 1)
     branch_3, normed_3 = send_y(branch_3, -1), send_z(normed_3, -1)
     (branch_0,) = branch_parts(pos, attended, out_weight, SIDE, [(0, 0)])
@@ -601,7 +583,9 @@
     gain_part = jnp.sum(normed_grad * own_unit, axis=0)
     sums = jnp.stack([gain_part, gate_part])
     sums = sums + send_core(sums)
-    sums = sums + send_x(sums, 1) + send_x(sums, -1) + send_x(sums, 2)
+    sums, query_weight_grad = hold(
+        sums + send_x(sums, 1) + send_x(sums, -1) + send_x(sums, 2), query_weight_grad
+    )
     return (
         layer_out,
         text_grad,

time: 220 us -> 219 us (level)
  Pallas kernels: 44.8 us -> 38.9 us
  other arithmetic: 12.6 us -> 17 us
    pallas_call x19 -> x18, Pallas kernels: 44.8 us -> 38.9 us  [call(): pl.pallas_call(body, grid_spec=pltpu.PrefetchScalarGridSpec(num_scalar_pr...]
    convert_element_type x0 -> x2, other arithmetic: none -> 4.12 us  [the longest x1 2.58 us: shards(): add(normed_1, normed_2).astype(BF)]
    unnamed x96 -> x98, local copies, waits for them, and re-layouts: 19.9 us -> 20.2 us
  transfers between devices with their start and end apart: 42 -> 42, of which waited for: 21 -> 19; matrix products, arithmetic and copies ran while one was open for 9% -> 11% of each run, Pallas kernels for 16% -> 13%
where the time goes in v2:
time: 219 us; the launch traced here: 218 us
  starting transfers between devices  52.2 us (24%)
  waiting for transfers between devices  49.2 us (22%)
  Pallas kernels  38.9 us (18%)
  local copies, waits for them, and re-layouts  29 us (13%)
  between operations  18.1 us (8%)
  other arithmetic  17 us (8%)
  blocking collectives  13.5 us (6%)
    ppermute x36, starting transfers between devices, ring_send(): return lax.ppermute(value, ('dp', 'tensor'), moves)  49.2 us
    ppermute x36, waiting for transfers between devices, ring_send(): return lax.ppermute(value, ('dp', 'tensor'), moves)  48 us
    pallas_call x18, Pallas kernels, call(): pl.pallas_call(body, grid_spec=pltpu.PrefetchScalarGridSpec(num_scalar_pr...  38.9 us
    unnamed x98, local copies, waits for them, and re-layouts  20.2 us
    all_gather x1, blocking collectives, shards(): pair = lax.all_gather(pair, 'dp', axis=0)  13.5 us
  transfers between devices with their start and end apart: 42, of which 19 were waited for; matrix products, arithmetic and copies ran while one was open for 11% of the time, Pallas kernels for 13%

profile of v2, /device:TPU:0, one launch (start us, length us, event | category | flops | bytes accessed | tf_op | source)
XLA Modules:
  0.0 217.9 jit_solution(8264270221167147009)
XLA Ops:
  9.0 3.2 %collective-permute-start.8 = (bf16[256,512]{1,0:T(8,128)(2,1)S(1)}, bf16[256,512]{1,0:T(8,128)(2,1)S(1)}, u32[]{:S(2)}, u32[]{:S(2)}) collective-permute-start(bf16[256,512]{1,0:T(8,128)(2,1)S(1)} %fusion.3), channel_id=1, source_target_pairs={{0,12},{1,13},{2,14},{3,15},{4,0},{5,1},{6,2},{7,3},{8,4},{9,5},{1... | collective-permute-start | bytes 786440 | tf_op jit(solution)/shard_map/ppermute | solution.py:42
  19.8 5.4 %collective-permute-done.1 = bf16[336,512]{1,0:T(8,128)(2,1)S(1)} collective-permute-done((bf16[336,512]{1,0:T(8,128)(2,1)S(1)}, bf16[336,512]{1,0:T(8,128)(2,1)S(1)}, u32[]{:S(2)}, u32[]{:S(2)}) %collective-permute-start.1) | collective-permute-done | bytes 344096 | tf_op jit(solution)/shard_map/ppermute | solution.py:42
  26.1 7.6 %collective-permute-done.2 = bf16[336,512]{1,0:T(8,128)(2,1)S(1)} collective-permute-done((bf16[336,512]{1,0:T(8,128)(2,1)S(1)}, bf16[336,512]{1,0:T(8,128)(2,1)S(1)}, u32[]{:S(2)}, u32[]{:S(2)}) %collective-permute-start.2) | collective-permute-done | bytes 344096 | tf_op jit(solution)/shard_map/ppermute | solution.py:42
  34.9 5.4 %collective-permute-start.4 = (bf16[4,80,512]{2,1,0:T(8,128)(2,1)S(1)}, bf16[4,80,512]{2,1,0:T(8,128)(2,1)S(1)}, u32[]{:S(2)}, u32[]{:S(2)}) collective-permute-start(bf16[4,80,512]{2,1,0:T(8,128)(2,1)S(1)} %pad_maximum_fusion.3.refs_1_.refs_0_), channel_id=1, source_target_pairs={{0,8},{1,9},{2,10},{3,11},{4,12},{5,13},{6,14},{7,15},{8,0},{9,1},... | collective-permute-start | bytes 983048 | tf_op jit(solution)/shard_map/ppermute | solution.py:42
  40.6 3.2 %collective-permute-start.11 = (bf16[4,256,512]{2,1,0:T(8,128)(2,1)S(1)}, bf16[4,256,512]{2,1,0:T(8,128)(2,1)S(1)}, u32[]{:S(2)}, u32[]{:S(2)}) collective-permute-start(bf16[4,256,512]{2,1,0:T(8,128)(2,1)S(1)} %pad_maximum_fusion.1.refs_0_), channel_id=1, source_target_pairs={{0,3},{1,0},{2,1},{3,2},{4,7},{5,4},{6,5},{7,6},{8,11},{9,8},{10,9... | collective-permute-start | bytes 3145736 | tf_op jit(solution)/shard_map/ppermute | solution.py:42
  46.4 3.6 %collective-permute-done.4.refs_2_.refs_1_ = bf16[4,80,512]{2,1,0:T(8,128)(2,1)S(1)} collective-permute-done((bf16[4,80,512]{2,1,0:T(8,128)(2,1)S(1)}, bf16[4,80,512]{2,1,0:T(8,128)(2,1)S(1)}, u32[]{:S(2)}, u32[]{:S(2)}) %collective-permute-start.4) | collective-permute-done | bytes 327712 | tf_op jit(solution)/shard_map/ppermute | solution.py:42
  50.0 3.2 %collective-permute-start.6 = (bf16[4,256,512]{2,1,0:T(8,128)(2,1)S(1)}, bf16[4,256,512]{2,1,0:T(8,128)(2,1)S(1)}, u32[]{:S(2)}, u32[]{:S(2)}) collective-permute-start(bf16[4,256,512]{2,1,0:T(8,128)(2,1)S(1)} %pad_maximum_fusion.refs_0_), channel_id=1, source_target_pairs={{0,12},{1,13},{2,14},{3,15},{4,0},{5,1},{6,2},{7,3},{8,4},{9,5},{1... | collective-permute-start | bytes 3145736 | tf_op jit(solution)/shard_map/ppermute | solution.py:42
  58.8 2.8 %shard_map.171 = bf16[64,512]{1,0:T(8,128)(2,1)S(1)} custom-call(s32[4]{0:T(128)S(1)} %pad_add_fusion.pos, bf16[4,80,512]{2,1,0:T(8,128)(2,1)S(1)} %pad_maximum_fusion.3.refs_1_.refs_0_, bf16[4,80,512]{2,1,0:T(8,128)(2,1)S(1)} %collective-permute-done.3.refs_1_.refs_2_, bf16[4,80,512]{2,1,0:T(8,128)(2,1)S(1)} %collective-permute-done.4.refs_2_.refs_1_, ...), custom_call_target="tpu_custom_call" | custom-call | flops 8388608 | bytes 163840 | tf_op jit(solution)/shard_map/pallas_call | solution.py:90
  61.6 13.5 %all-gather = bf16[512,512]{1,0:T(8,128)(2,1)S(1)} all-gather(bf16[64,512]{1,0:T(8,128)(2,1)S(1)} %shard_map.171), channel_id=2, replica_groups=mesh['dp'=8,'tensor'=16] {'dp'}, dimensions={0}, use_global_device_ids=true | all-gather | bytes 589824 | tf_op jit(solution)/shard_map/all_gather | solution.py:478
  86.1 4.5 %collective-permute-done.17.refs_2_ = bf16[2,64,1024]{2,1,0:T(8,128)(2,1)S(1)} collective-permute-done((bf16[2,64,1024]{2,1,0:T(8,128)(2,1)S(1)}, bf16[2,64,1024]{2,1,0:T(8,128)(2,1)S(1)}, u32[]{:S(2)}, u32[]{:S(2)}) %collective-permute-start.17) | collective-permute-done | bytes 262176 | tf_op jit(solution)/shard_map/ppermute | solution.py:42
  95.0 2.9 %shard_map.178 = (bf16[256,256]{1,0:T(8,128)(2,1)S(1)}, bf16[256,256]{1,0:T(8,128)(2,1)S(1)}, bf16[256,256]{1,0:T(8,128)(2,1)S(1)}, bf16[4,64,512]{2,1,0:T(8,128...) custom-call(s32[12]{0:T(128)S(1)} %concatenate.38.pos, ...), custom_call_target="tpu_custom_call" | custom-call | flops 5242880 | bytes 49152 | tf_op jit(solution)/shard_map/pallas_call | solution.py:90
  100.7 3.0 %shard_map.185 = bf16[4,2,1024,256]{3,2,1,0:T(8,128)(2,1)S(1)} custom-call(s32[4]{0:T(128)S(1)} %pad_add_fusion.pos, bf16[256,256]{1,0:T(8,128)(2,1)S(1)} %get-tuple-element.139.query_grad, bf16[4,256,512]{2,1,0:T(8,128)(2,1)S(1)} %pad_maximum_fusion.refs_0_, bf16[4,256,512]{2,1,0:T(8,128)(2,1)S(1)} %collective-permute-done.6.refs_0_.refs_1_, ...), custom_call_target="tpu_custom_call" | custom-call | flops 16777216 | bytes 131072 | tf_op jit(solution)/shard_map/pallas_call | solution.py:90
  113.4 2.7 %collective-permute-start.19 = (bf16[4,64,512]{2,1,0:T(8,128)(2,1)S(1)}, bf16[4,64,512]{2,1,0:T(8,128)(2,1)S(1)}, u32[]{:S(2)}, u32[]{:S(2)}) collective-permute-start(bf16[4,64,512]{2,1,0:T(8,128)(2,1)S(1)} %copy-done.38), channel_id=1, source_target_pairs={{0,16},{16,0},{32,48},{48,32},{64,80},{80,64},{96,112},{112,96},{1... | collective-permute-start | bytes 786440 | tf_op jit(solution)/shard_map/ppermute | solution.py:51
  124.0 3.2 %collective-permute-start.22 = (bf16[4,64,512]{2,1,0:T(8,128)(2,1)S(1)}, bf16[4,64,512]{2,1,0:T(8,128)(2,1)S(1)}, u32[]{:S(2)}, u32[]{:S(2)}) collective-permute-start(bf16[4,64,512]{2,1,0:T(8,128)(2,1)S(1)} %add_convert_fusion.9), channel_id=1, source_target_pairs={{0,96},{1,97},{2,98},{3,99},{4,100},{5,101},{6,102},{7,103},{8,104... | collective-permute-start | bytes 786440 | tf_op jit(solution)/shard_map/ppermute | solution.py:42
  129.5 3.2 %shard_map.181 = (bf16[4,256,512]{2,1,0:T(8,128)(2,1)S(1)}, bf16[4,256,512]{2,1,0:T(8,128)(2,1)}) custom-call(s32[4]{0:T(128)S(1)} %pad_add_fusion.pos, bf16[256,256]{1,0:T(8,128)(2,1)S(1)} %copy-done.21, bf16[256,8192]{1,0:T(8,128)(2,1)S(1)} %copy-done.4, bf16[256,8192]{1,0:T(8,128)(2,1)S(1)} %copy-done.4), custom_call_target="tpu_custom_call" | custom-call | flops 8388608 | bytes 65536 | tf_op jit(solution)/shard_map/pallas_call | solution.py:90
  132.7 3.1 %shard_map.182 = (bf16[4,272,512]{2,1,0:T(8,128)(2,1)S(1)}, bf16[4,272,512]{2,1,0:T(8,128)(2,1)}) custom-call(s32[4]{0:T(128)S(1)} %pad_add_fusion.pos, bf16[256,256]{1,0:T(8,128)(2,1)S(1)} %copy-done.23, bf16[8192,256]{1,0:T(8,128)(2,1)S(1)} %copy-done.8, bf16[8192,256]{1,0:T(8,128)(2,1)S(1)} %copy-done.8, bf16[16,512]{1,0:T(8,128)(2,1)S(1)} %copy-done.36), custom_call_target="tpu_custom_call" | custom-call | flops 8388608 | bytes 65536 | tf_op jit(solution)/shard_map/pallas_call | solution.py:90
  135.7 2.7 %collective-permute-done.20 = bf16[4,256,512]{2,1,0:T(8,128)(2,1)} collective-permute-done((bf16[4,256,512]{2,1,0:T(8,128)(2,1)S(1)}, bf16[4,256,512]{2,1,0:T(8,128)(2,1)}, u32[]{:S(2)}, u32[]{:S(2)}) %collective-permute-start.20) | collective-permute-done | bytes 1048608 | tf_op jit(solution)/shard_map/ppermute | solution.py:42
  140.0 2.6 %add_convert_fusion = bf16[4,272,512]{2,1,0:T(8,128)(2,1)} fusion(bf16[4,272,512]{2,1,0:T(8,128)(2,1)} %collective-permute-done.21, bf16[4,272,512]{2,1,0:T(8,128)(2,1)S(1)} %get-tuple-element.120), kind=kLoop, calls=%fused_computation.1 | loop fusion | flops 2228224 | bytes 3342336 | tf_op jit(solution)/shard_map/convert_element_type | solution.py:549
  147.5 2.9 %collective-permute-start.27 = (bf16[4,272,512]{2,1,0:T(8,128)(2,1)}, bf16[4,272,512]{2,1,0:T(8,128)(2,1)}, u32[]{:S(2)}, u32[]{:S(2)}) collective-permute-start(bf16[4,272,512]{2,1,0:T(8,128)(2,1)} %get-tuple-element.129), channel_id=1, source_target_pairs={{0,3},{1,0},{2,1},{3,2},{4,7},{5,4},{6,5},{7,6},{8,11},{9,8},{10,9... | collective-permute-start | bytes 3342344 | tf_op jit(solution)/shard_map/ppermute | solution.py:42
  166.0 4.6 %collective-permute-done.24 = bf16[4,256,512]{2,1,0:T(8,128)(2,1)} collective-permute-done((bf16[4,256,512]{2,1,0:T(8,128)(2,1)S(1)}, bf16[4,256,512]{2,1,0:T(8,128)(2,1)}, u32[]{:S(2)}, u32[]{:S(2)}) %collective-permute-start.24) | collective-permute-done | bytes 1048608 | tf_op jit(solution)/shard_map/ppermute | solution.py:42
  170.6 4.8 %collective-permute-done.26 = bf16[4,272,512]{2,1,0:T(8,128)(2,1)S(1)} collective-permute-done((bf16[4,272,512]{2,1,0:T(8,128)(2,1)}, bf16[4,272,512]{2,1,0:T(8,128)(2,1)S(1)}, u32[]{:S(2)}, u32[]{:S(2)}) %collective-permute-start.26) | collective-permute-done | bytes 1114144 | tf_op jit(solution)/shard_map/ppermute | solution.py:42
  184.0 3.9 %collective-permute-done.30 = bf16[256,512]{1,0:T(8,128)(2,1)S(1)} collective-permute-done((bf16[256,512]{1,0:T(8,128)(2,1)S(1)}, bf16[256,512]{1,0:T(8,128)(2,1)S(1)}, u32[]{:S(2)}, u32[]{:S(2)}) %collective-permute-start.30) | collective-permute-done | bytes 262176 | tf_op jit(solution)/shard_map/ppermute | solution.py:42
  189.0 2.8 %collective-permute-done.31 = bf16[256,512]{1,0:T(8,128)(2,1)S(1)} collective-permute-done((bf16[256,512]{1,0:T(8,128)(2,1)S(1)}, bf16[256,512]{1,0:T(8,128)(2,1)S(1)}, u32[]{:S(2)}, u32[]{:S(2)}) %collective-permute-start.31) | collective-permute-done | bytes 262176 | tf_op jit(solution)/shard_map/ppermute | solution.py:42
  193.9 2.6 %collective-permute-done.35 = bf16[272,512]{1,0:T(8,128)(2,1)S(1)} collective-permute-done((bf16[272,512]{1,0:T(8,128)(2,1)S(1)}, bf16[272,512]{1,0:T(8,128)(2,1)S(1)}, u32[]{:S(2)}, u32[]{:S(2)}) %collective-permute-start.35) | collective-permute-done | bytes 278560 | tf_op jit(solution)/shard_map/ppermute | solution.py:42
  (235 shorter events, 102.6 us)
Async XLA Ops:
  7.2 201.2 %reduce-scatter.3.cloned.1.call-start = ((), (), s32[]{:S(2)}) async-start(), calls=%async_computation.2 | async-start | bytes 4718592 | tf_op jit(solution)/shard_map/reduce_scatter | solution.py:531
  9.0 31.4 %collective-permute-start.8 = (bf16[256,512]{1,0:T(8,128)(2,1)S(1)}, bf16[256,512]{1,0:T(8,128)(2,1)S(1)}, u32[]{:S(2)}, u32[]{:S(2)}) collective-permute-start(bf16[256,512]{1,0:T(8,128)(2,1)S(1)} %fusion.3), channel_id=1, source_target_pairs={{0,12},{1,13},{2,14},{3,15},{4,0},{5,1},{6,2},{7,3},{8,4},{9,5},{1... | collective-permute-start | bytes 786440 | tf_op jit(solution)/shard_map/ppermute | solution.py:42
  19.7 20.7 %collective-permute-start.10 = (bf16[256,512]{1,0:T(8,128)(2,1)S(1)}, bf16[256,512]{1,0:T(8,128)(2,1)S(1)}, u32[]{:S(2)}, u32[]{:S(2)}) collective-permute-start(bf16[256,512]{1,0:T(8,128)(2,1)S(1)} %collective-permute-done.9), channel_id=1, source_target_pairs={{0,4},{1,5},{2,6},{3,7},{4,8},{5,9},{6,10},{7,11},{8,12},{9,13},{1... | collective-permute-start | bytes 786440 | tf_op jit(solution)/shard_map/ppermute | solution.py:42
  34.9 15.0 %collective-permute-start.4 = (bf16[4,80,512]{2,1,0:T(8,128)(2,1)S(1)}, bf16[4,80,512]{2,1,0:T(8,128)(2,1)S(1)}, u32[]{:S(2)}, u32[]{:S(2)}) collective-permute-start(bf16[4,80,512]{2,1,0:T(8,128)(2,1)S(1)} %pad_maximum_fusion.3.refs_1_.refs_0_), channel_id=1, source_target_pairs={{0,8},{1,9},{2,10},{3,11},{4,12},{5,13},{6,14},{7,15},{8,0},{9,1},... | collective-permute-start | bytes 983048 | tf_op jit(solution)/shard_map/ppermute | solution.py:42
  40.5 34.6 %collective-permute-start.12 = (bf16[4,256,512]{2,1,0:T(8,128)(2,1)S(1)}, bf16[4,256,512]{2,1,0:T(8,128)(2,1)S(1)}, u32[]{:S(2)}, u32[]{:S(2)}) collective-permute-start(bf16[4,256,512]{2,1,0:T(8,128)(2,1)S(1)} %pad_maximum_fusion.1.refs_0_), channel_id=1, source_target_pairs={{0,1},{1,2},{2,3},{3,0},{4,5},{5,6},{6,7},{7,4},{8,9},{9,10},{10,1... | collective-permute-start | bytes 3145736 | tf_op jit(solution)/shard_map/ppermute | solution.py:42
  40.6 34.5 %collective-permute-start.11 = (bf16[4,256,512]{2,1,0:T(8,128)(2,1)S(1)}, bf16[4,256,512]{2,1,0:T(8,128)(2,1)S(1)}, u32[]{:S(2)}, u32[]{:S(2)}) collective-permute-start(bf16[4,256,512]{2,1,0:T(8,128)(2,1)S(1)} %pad_maximum_fusion.1.refs_0_), channel_id=1, source_target_pairs={{0,3},{1,0},{2,1},{3,2},{4,7},{5,4},{6,5},{7,6},{8,11},{9,8},{10,9... | collective-permute-start | bytes 3145736 | tf_op jit(solution)/shard_map/ppermute | solution.py:42
  49.9 25.2 %collective-permute-start.7 = (bf16[4,256,512]{2,1,0:T(8,128)(2,1)S(1)}, bf16[4,256,512]{2,1,0:T(8,128)(2,1)S(1)}, u32[]{:S(2)}, u32[]{:S(2)}) collective-permute-start(bf16[4,256,512]{2,1,0:T(8,128)(2,1)S(1)} %pad_maximum_fusion.refs_0_), channel_id=1, source_target_pairs={{0,4},{1,5},{2,6},{3,7},{4,8},{5,9},{6,10},{7,11},{8,12},{9,13},{1... | collective-permute-start | bytes 3145736 | tf_op jit(solution)/shard_map/ppermute | solution.py:42
  50.0 25.1 %collective-permute-start.6 = (bf16[4,256,512]{2,1,0:T(8,128)(2,1)S(1)}, bf16[4,256,512]{2,1,0:T(8,128)(2,1)S(1)}, u32[]{:S(2)}, u32[]{:S(2)}) collective-permute-start(bf16[4,256,512]{2,1,0:T(8,128)(2,1)S(1)} %pad_maximum_fusion.refs_0_), channel_id=1, source_target_pairs={{0,12},{1,13},{2,14},{3,15},{4,0},{5,1},{6,2},{7,3},{8,4},{9,5},{1... | collective-permute-start | bytes 3145736 | tf_op jit(solution)/shard_map/ppermute | solution.py:42
  54.3 20.8 %collective-permute-start.13 = (bf16[4,64,1024]{2,1,0:T(8,128)(2,1)S(1)}, bf16[4,64,1024]{2,1,0:T(8,128)(2,1)S(1)}, u32[]{:S(2)}, u32[]{:S(2)}) collective-permute-start(bf16[4,64,1024]{2,1,0:T(8,128)(2,1)S(1)} %get-tuple-element.90), channel_id=1, source_target_pairs={{0,16},{16,0},{32,48},{48,32},{64,80},{80,64},{96,112},{112,96},{1... | collective-permute-start | bytes 1572872 | tf_op jit(solution)/shard_map/ppermute | solution.py:51
  75.1 16.1 %collective-permute-start.14 = (bf16[4,256,512]{2,1,0:T(8,128)(2,1)S(1)}, bf16[4,256,512]{2,1,0:T(8,128)(2,1)S(1)}, u32[]{:S(2)}, u32[]{:S(2)}) collective-permute-start(bf16[4,256,512]{2,1,0:T(8,128)(2,1)S(1)} %collective-permute-done.7.refs_1_.refs_3_), channel_id=1, source_target_pairs={{0,4},{1,5},{2,6},{3,7},{4,8},{5,9},{6,10},{7,11},{8,12},{9,13},{1... | collective-permute-start | bytes 3145736 | tf_op jit(solution)/shard_map/ppermute | solution.py:42
  75.2 16.2 %collective-permute-start.15 = (bf16[4,256,512]{2,1,0:T(8,128)(2,1)S(1)}, bf16[4,256,512]{2,1,0:T(8,128)(2,1)S(1)}, u32[]{:S(2)}, u32[]{:S(2)}) collective-permute-start(bf16[4,256,512]{2,1,0:T(8,128)(2,1)S(1)} %collective-permute-done.12.refs_1_.refs_3_), channel_id=1, source_target_pairs={{0,1},{1,2},{2,3},{3,0},{4,5},{5,6},{6,7},{7,4},{8,9},{9,10},{10,1... | collective-permute-start | bytes 3145736 | tf_op jit(solution)/shard_map/ppermute | solution.py:42
  105.8 105.3 %reduce-scatter.5.cloned.1.call-start = ((), (), s32[]{:S(2)}) async-start(), calls=%async_computation.3 | async-start | bytes 4718592 | tf_op jit(solution)/shard_map/reduce_scatter | solution.py:531
  122.3 16.2 %collective-permute-start.20 = (bf16[4,256,512]{2,1,0:T(8,128)(2,1)S(1)}, bf16[4,256,512]{2,1,0:T(8,128)(2,1)}, u32[]{:S(2)}, u32[]{:S(2)}) collective-permute-start(bf16[4,256,512]{2,1,0:T(8,128)(2,1)S(1)} %shard_map.179), channel_id=1, source_target_pairs={{0,4},{1,5},{2,6},{3,7},{4,8},{5,9},{6,10},{7,11},{8,12},{9,13},{1... | collective-permute-start | bytes 3145736 | tf_op jit(solution)/shard_map/ppermute | solution.py:42
  122.4 17.6 %collective-permute-start.21 = (bf16[4,272,512]{2,1,0:T(8,128)(2,1)S(1)}, bf16[4,272,512]{2,1,0:T(8,128)(2,1)}, u32[]{:S(2)}, u32[]{:S(2)}) collective-permute-start(bf16[4,272,512]{2,1,0:T(8,128)(2,1)S(1)} %shard_map.180), channel_id=1, source_target_pairs={{0,1},{1,2},{2,3},{3,0},{4,5},{5,6},{6,7},{7,4},{8,9},{9,10},{10,1... | collective-permute-start | bytes 3342344 | tf_op jit(solution)/shard_map/ppermute | solution.py:42
  124.0 18.6 %collective-permute-start.23 = (bf16[4,64,512]{2,1,0:T(8,128)(2,1)S(1)}, bf16[4,64,512]{2,1,0:T(8,128)(2,1)S(1)}, u32[]{:S(2)}, u32[]{:S(2)}) collective-permute-start(bf16[4,64,512]{2,1,0:T(8,128)(2,1)S(1)} %add_convert_fusion.9), channel_id=1, source_target_pairs={{0,32},{1,33},{2,34},{3,35},{4,36},{5,37},{6,38},{7,39},{8,40},{9,... | collective-permute-start | bytes 786440 | tf_op jit(solution)/shard_map/ppermute | solution.py:42
  124.0 18.6 %collective-permute-start.22 = (bf16[4,64,512]{2,1,0:T(8,128)(2,1)S(1)}, bf16[4,64,512]{2,1,0:T(8,128)(2,1)S(1)}, u32[]{:S(2)}, u32[]{:S(2)}) collective-permute-start(bf16[4,64,512]{2,1,0:T(8,128)(2,1)S(1)} %add_convert_fusion.9), channel_id=1, source_target_pairs={{0,96},{1,97},{2,98},{3,99},{4,100},{5,101},{6,102},{7,103},{8,104... | collective-permute-start | bytes 786440 | tf_op jit(solution)/shard_map/ppermute | solution.py:42
  142.6 15.9 %collective-permute-start.28 = (bf16[4,64,512]{2,1,0:T(8,128)(2,1)S(1)}, bf16[4,64,512]{2,1,0:T(8,128)(2,1)}, u32[]{:S(2)}, u32[]{:S(2)}) collective-permute-start(bf16[4,64,512]{2,1,0:T(8,128)(2,1)S(1)} %add_convert_fusion.9), channel_id=1, source_target_pairs={{0,64},{1,65},{2,66},{3,67},{4,68},{5,69},{6,70},{7,71},{8,72},{9,... | collective-permute-start | bytes 786440 | tf_op jit(solution)/shard_map/ppermute | solution.py:42
  144.0 26.6 %collective-permute-start.24 = (bf16[4,256,512]{2,1,0:T(8,128)(2,1)S(1)}, bf16[4,256,512]{2,1,0:T(8,128)(2,1)}, u32[]{:S(2)}, u32[]{:S(2)}) collective-permute-start(bf16[4,256,512]{2,1,0:T(8,128)(2,1)S(1)} %add_convert_fusion.1), channel_id=1, source_target_pairs={{0,4},{1,5},{2,6},{3,7},{4,8},{5,9},{6,10},{7,11},{8,12},{9,13},{1... | collective-permute-start | bytes 3145736 | tf_op jit(solution)/shard_map/ppermute | solution.py:42
  145.6 25.0 %collective-permute-start.25 = (bf16[4,256,512]{2,1,0:T(8,128)(2,1)}, bf16[4,256,512]{2,1,0:T(8,128)(2,1)}, u32[]{:S(2)}, u32[]{:S(2)}) collective-permute-start(bf16[4,256,512]{2,1,0:T(8,128)(2,1)} %get-tuple-element.126), channel_id=1, source_target_pairs={{0,12},{1,13},{2,14},{3,15},{4,0},{5,1},{6,2},{7,3},{8,4},{9,5},{1... | collective-permute-start | bytes 3145736 | tf_op jit(solution)/shard_map/ppermute | solution.py:42
  147.2 28.2 %collective-permute-start.26 = (bf16[4,272,512]{2,1,0:T(8,128)(2,1)}, bf16[4,272,512]{2,1,0:T(8,128)(2,1)S(1)}, u32[]{:S(2)}, u32[]{:S(2)}) collective-permute-start(bf16[4,272,512]{2,1,0:T(8,128)(2,1)} %add_convert_fusion), channel_id=1, source_target_pairs={{0,1},{1,2},{2,3},{3,0},{4,5},{5,6},{6,7},{7,4},{8,9},{9,10},{10,1... | collective-permute-start | bytes 3342344 | tf_op jit(solution)/shard_map/ppermute | solution.py:42
  147.5 27.9 %collective-permute-start.27 = (bf16[4,272,512]{2,1,0:T(8,128)(2,1)}, bf16[4,272,512]{2,1,0:T(8,128)(2,1)}, u32[]{:S(2)}, u32[]{:S(2)}) collective-permute-start(bf16[4,272,512]{2,1,0:T(8,128)(2,1)} %get-tuple-element.129), channel_id=1, source_target_pairs={{0,3},{1,0},{2,1},{3,2},{4,7},{5,4},{6,5},{7,6},{8,11},{9,8},{10,9... | collective-permute-start | bytes 3342344 | tf_op jit(solution)/shard_map/ppermute | solution.py:42
  178.9 12.8 %collective-permute-start.31 = (bf16[256,512]{1,0:T(8,128)(2,1)S(1)}, bf16[256,512]{1,0:T(8,128)(2,1)S(1)}, u32[]{:S(2)}, u32[]{:S(2)}) collective-permute-start(bf16[256,512]{1,0:T(8,128)(2,1)S(1)} %get-tuple-element.159), channel_id=1, source_target_pairs={{0,1},{1,2},{2,3},{3,0},{4,5},{5,6},{6,7},{7,4},{8,9},{9,10},{10,1... | collective-permute-start | bytes 786440 | tf_op jit(solution)/shard_map/ppermute | solution.py:42
  180.8 13.1 %collective-permute-start.33 = (bf16[272,512]{1,0:T(8,128)(2,1)S(1)}, bf16[272,512]{1,0:T(8,128)(2,1)S(1)}, u32[]{:S(2)}, u32[]{:S(2)}) collective-permute-start(bf16[272,512]{1,0:T(8,128)(2,1)S(1)} %get-tuple-element.154), channel_id=1, source_target_pairs={{0,8},{1,9},{2,10},{3,11},{4,12},{5,13},{6,14},{7,15},{8,0},{9,1},... | collective-permute-start | bytes 835592 | tf_op jit(solution)/shard_map/ppermute | solution.py:42
  182.0 14.5 %collective-permute-start.35 = (bf16[272,512]{1,0:T(8,128)(2,1)S(1)}, bf16[272,512]{1,0:T(8,128)(2,1)S(1)}, u32[]{:S(2)}, u32[]{:S(2)}) collective-permute-start(bf16[272,512]{1,0:T(8,128)(2,1)S(1)} %get-tuple-element.155), channel_id=1, source_target_pairs={{0,12},{1,13},{2,14},{3,15},{4,0},{5,1},{6,2},{7,3},{8,4},{9,5},{1... | collective-permute-start | bytes 835592 | tf_op jit(solution)/shard_map/ppermute | solution.py:42
  (66 other events, 487.6 us)
Sparse Core Ops, SparseCore 0:
  105.9 48.0 reduce-scatter.2
  157.0 37.2 reduce-scatter.4
